TPU v7x, 256 devices: a whole 4x4x8 slice. The times are simulated.
256 devices in a mesh: section: 8 (over x_hi, y), peer: 16 (over x_lo, z), shard: 2 (over core).
Axes of the slice: x: 4 (x_hi: 2, x_lo: 2; x = x_hi * 2 + x_lo), y: 4, z: 8, core: 2. Of those that a mesh axis runs over, the one named last changes fastest.
Arguments:
- forward_rows: bfloat16 [32768, 5120], P(('section', 'peer', 'shard')), may hold values from -6 to 6
- saved_rows: bfloat16 [32768, 5120], P(('section', 'peer', 'shard')), may hold values from -6 to 6
- output_grad: bfloat16 [32768, 5120], P(('section', 'peer', 'shard')), may hold values from -6 to 6
- norm_gain: bfloat16 [8, 5120], P('section'), may hold values from 0.5 to 2
- forward_counts: int32 [256, 16], P(('section', 'peer', 'shard')), may hold values from 0 to 16, as said below
- return_counts: int32 [256, 16], P(('section', 'peer', 'shard')), may hold values from 0 to 16, as said below
- matching: int32 [8, 16], P('section'), may hold values from 0 to 15, as said below
- down_weight: float32 [4096, 5120], P(('section', 'peer', 'shard')), may hold values from -0.078125 to 0.078125
- up_weight: float32 [4096, 5120], P(('section', 'peer', 'shard')), may hold values from -1 to 1
- down_moment: float32 [4096, 5120], P(('section', 'peer', 'shard')), may hold values from -60 to 60
- up_moment: float32 [4096, 5120], P(('section', 'peer', 'shard')), may hold values from -18 to 18
- down_square: float32 [4096, 5120], P(('section', 'peer', 'shard')), may hold values from 3 to 30
- up_square: float32 [4096, 5120], P(('section', 'peer', 'shard')), may hold values from 0.03 to 0.3
Outputs:
- arrived_rows: bfloat16 [65536, 5120], P(('section', 'peer', 'shard'))
- returned_grad: bfloat16 [65536, 5120], P(('section', 'peer', 'shard'))
- new_down_weight: float32 [4096, 5120], P(('section', 'peer', 'shard'))
- new_up_weight: float32 [4096, 5120], P(('section', 'peer', 'shard'))
- new_down_moment: float32 [4096, 5120], P(('section', 'peer', 'shard'))
- new_up_moment: float32 [4096, 5120], P(('section', 'peer', 'shard'))
- new_down_square: float32 [4096, 5120], P(('section', 'peer', 'shard'))
- new_up_square: float32 [4096, 5120], P(('section', 'peer', 'shard'))
Inputs may be any that keep to these rules, and one draw needn't show every extreme that they name: `forward_counts`: each row sums to 128 and no entry exceeds 16. In every section one peer receives exactly 16 rows from every device of that section, so that its slots are full from every sender. `return_counts`: each row sums to 128 and no entry exceeds 16. In every section one peer of the previous section is sent exactly 16 rows by every device of that section. Each row pairs the 16 peers of a section: matching[s, p] = q exactly when matching[s, q] = p, and q differs from p.
All inputs are finite; a program needn't handle non-finite values.
Results may differ from a plain program's by a relative error of at most 0.0062.
Values may be sent and summed in bfloat16 or wider, within the bound.
A program may use at most 128 MiB of HBM per device.

v0:
```python
import jax
import jax.numpy as jnp
from jax import lax
from jax.sharding import PartitionSpec as P

lane_width = 128
beta_one = 0.9
beta_two = 0.999
learn_rate = 0.001
adam_eps = 1e-08
norm_eps = 1e-05
step_count = 20


def shifted(block, axis, distance):
    devices = range(lax.axis_size(axis))
    route = [(i - distance, i) for i in devices if i - distance in devices]
    return lax.ppermute(block, axis, route)


def rms_inverse(values):
    widened = values.astype(jnp.float32)
    return 1.0 / jnp.sqrt(jnp.mean(widened * widened, axis=-1, keepdims=True) + norm_eps)


def silu_slope(pre_value):
    sigmoid = jax.nn.sigmoid(pre_value)
    return sigmoid * (1.0 + pre_value * (1.0 - sigmoid))


def adam_update(weight, moment, second, gradient):
    moment_new = beta_one * moment + (1.0 - beta_one) * gradient
    second_new = beta_two * second + (1.0 - beta_two) * gradient * gradient
    first_fix = 1.0 - beta_one**step_count
    second_fix = 1.0 - beta_two**step_count
    weight_new = weight - learn_rate * (moment_new / first_fix) / (
        jnp.sqrt(second_new / second_fix) + adam_eps
    )
    return (weight_new, moment_new, second_new)


def pack_slots(values, counts, capacity):
    peer_total = counts.shape[-1]
    per_peer = counts.reshape(peer_total)
    offsets = jnp.cumsum(per_peer) - per_peer
    slot_index = lax.broadcasted_iota(jnp.int32, (peer_total, capacity), 1)
    live_slot = slot_index < per_peer[:, None]
    source_row = jnp.where(live_slot, offsets[:, None] + slot_index, 0).reshape(
        peer_total * capacity
    )
    picked = jnp.take(values, source_row, axis=0)
    return jnp.where(live_slot.reshape(peer_total * capacity, 1), picked, jnp.zeros_like(picked))


def norm_rows(values, gain_wide):
    return (values.astype(jnp.float32) * rms_inverse(values) * gain_wide).astype(jnp.bfloat16)


def local(
    forward_rows,
    saved_rows,
    output_grad,
    norm_gain,
    forward_counts,
    return_counts,
    matching,
    down_weight,
    up_weight,
    down_moment,
    up_moment,
    down_square,
    up_square,
):
    gain_wide = norm_gain.astype(jnp.float32)
    down_bf = down_weight.astype(jnp.bfloat16)
    up_bf = up_weight.astype(jnp.bfloat16)
    own_rows = forward_rows.shape[0]
    all_forward, all_saved, all_grad = (
        lax.all_gather(forward_rows, "shard", axis=0, tiled=True),
        lax.all_gather(saved_rows, "shard", axis=0, tiled=True),
        lax.all_gather(output_grad, "shard", axis=0, tiled=True),
    )
    act_forward = jax.nn.silu(
        jnp.dot(norm_rows(all_forward, gain_wide), down_bf.T, preferred_element_type=jnp.float32)
    ).astype(jnp.bfloat16)
    branch_out = lax.psum_scatter(
        jnp.dot(act_forward, up_bf, preferred_element_type=jnp.float32),
        "shard",
        scatter_dimension=0,
        tiled=True,
    )
    normed_saved = norm_rows(all_saved, gain_wide)
    pre_saved = jnp.dot(normed_saved, down_bf.T, preferred_element_type=jnp.float32)
    act_saved = jax.nn.silu(pre_saved).astype(jnp.bfloat16)
    grad_act = jnp.dot(all_grad, up_bf.T, preferred_element_type=jnp.float32)
    grad_pre = (grad_act * silu_slope(pre_saved)).astype(jnp.bfloat16)
    grad_normed = lax.psum_scatter(
        jnp.dot(grad_pre, down_bf, preferred_element_type=jnp.float32),
        "shard",
        scatter_dimension=0,
        tiled=True,
    )
    grad_up = jnp.einsum("rk,rd->kd", act_saved, all_grad, preferred_element_type=jnp.float32)
    grad_down = jnp.einsum("rk,rd->kd", grad_pre, normed_saved, preferred_element_type=jnp.float32)
    block_out = (forward_rows.astype(jnp.float32) + branch_out).astype(jnp.bfloat16)
    saved_wide = saved_rows.astype(jnp.float32)
    saved_inv = rms_inverse(saved_rows)
    scaled = grad_normed * gain_wide
    inner = jnp.sum(scaled * saved_wide, axis=-1, keepdims=True)
    grad_in = (
        output_grad.astype(jnp.float32)
        + scaled * saved_inv
        - saved_wide * (saved_inv * saved_inv * saved_inv) * inner / saved_rows.shape[-1]
    ).astype(jnp.bfloat16)
    peer_total = lax.axis_size("peer")
    capacity = 2 * own_rows // peer_total
    packed_out = pack_slots(block_out, forward_counts, capacity)
    sorted_out = lax.all_to_all(packed_out, "peer", split_axis=0, concat_axis=0, tiled=True)
    arrived_rows = shifted(sorted_out, "section", 1)
    packed_grad = pack_slots(grad_in, return_counts, capacity)
    sorted_grad = lax.all_to_all(packed_grad, "peer", split_axis=0, concat_axis=0, tiled=True)
    returned_grad = shifted(sorted_grad, "section", -1)
    new_down = adam_update(down_weight, down_moment, down_square, grad_down)
    new_up = adam_update(up_weight, up_moment, up_square, grad_up)
    states = [new_down[0], new_up[0], new_down[1], new_up[1], new_down[2], new_up[2]]
    flat_items = [param_state.reshape(-1, lane_width) for param_state in states]
    spread = (
        lax.all_to_all(flat_items[0], "peer", split_axis=0, concat_axis=0, tiled=True),
        lax.all_to_all(flat_items[1], "peer", split_axis=0, concat_axis=0, tiled=True),
        lax.all_to_all(flat_items[2], "peer", split_axis=0, concat_axis=0, tiled=True),
        lax.all_to_all(flat_items[3], "peer", split_axis=0, concat_axis=0, tiled=True),
        lax.all_to_all(flat_items[4], "peer", split_axis=0, concat_axis=0, tiled=True),
        lax.all_to_all(flat_items[5], "peer", split_axis=0, concat_axis=0, tiled=True),
    )
    partner_ids = matching.reshape(peer_total)
    averaged = []
    for slab_rows in spread:
        blocks = slab_rows.reshape(peer_total, -1, lane_width)
        partner = jnp.take(blocks, partner_ids, axis=0)
        averaged.append(((blocks + partner) * 0.5).reshape(-1, lane_width))
    returned_states = (
        lax.all_to_all(averaged[0], "peer", split_axis=0, concat_axis=0, tiled=True),
        lax.all_to_all(averaged[1], "peer", split_axis=0, concat_axis=0, tiled=True),
        lax.all_to_all(averaged[2], "peer", split_axis=0, concat_axis=0, tiled=True),
        lax.all_to_all(averaged[3], "peer", split_axis=0, concat_axis=0, tiled=True),
        lax.all_to_all(averaged[4], "peer", split_axis=0, concat_axis=0, tiled=True),
        lax.all_to_all(averaged[5], "peer", split_axis=0, concat_axis=0, tiled=True),
    )
    finals = [flat_state.reshape(down_weight.shape) for flat_state in returned_states]
    return (
        arrived_rows,
        returned_grad,
        finals[0],
        finals[1],
        finals[2],
        finals[3],
        finals[4],
        finals[5],
    )


def solution(mesh):
    return jax.shard_map(
        local,
        mesh=mesh,
        in_specs=(
            P(("section", "peer", "shard"), None),
            P(("section", "peer", "shard"), None),
            P(("section", "peer", "shard"), None),
            P("section", None),
            P(("section", "peer", "shard"), None),
            P(("section", "peer", "shard"), None),
            P("section", None),
            P(("section", "peer", "shard"), None),
            P(("section", "peer", "shard"), None),
            P(("section", "peer", "shard"), None),
            P(("section", "peer", "shard"), None),
            P(("section", "peer", "shard"), None),
            P(("section", "peer", "shard"), None),
        ),
        out_specs=(
            P(("section", "peer", "shard"), None),
            P(("section", "peer", "shard"), None),
            P(("section", "peer", "shard"), None),
            P(("section", "peer", "shard"), None),
            P(("section", "peer", "shard"), None),
            P(("section", "peer", "shard"), None),
            P(("section", "peer", "shard"), None),
            P(("section", "peer", "shard"), None),
        ),
        check_vma=False,
    )
```

profile of v0, /device:TPU:56, one launch (start us, length us, event | category | flops | bytes accessed | tf_op | source)
XLA Modules:
  0.0 466.1 jit_solution(11938981425915379242)
XLA Ops:
  9.5 19.4 %all-gather.8.cloned.1.call-done = bf16[256,5120]{1,0:T(8,128)(2,1)} async-done(((bf16[128,5120]{1,0:T(8,128)(2,1)}), bf16[256,5120]{1,0:T(8,128)(2,1)}) %all-gather.8.cloned.1.call-update) | async-done | bytes 2621456 | tf_op jit(solution)/shard_map/all_gather | solution.py:80
  32.3 16.4 %all-gather.6.cloned.1.call-done = bf16[256,5120]{1,0:T(8,128)(2,1)} async-done(((bf16[128,5120]{1,0:T(8,128)(2,1)}), bf16[256,5120]{1,0:T(8,128)(2,1)}) %all-gather.6.cloned.1.call-update) | async-done | bytes 2621456 | tf_op jit(solution)/shard_map/all_gather | solution.py:81
  51.2 3.2 fusion.45
  54.5 14.0 %all-gather.4.cloned.1.call-done = bf16[256,5120]{1,0:T(8,128)(2,1)} async-done(((bf16[128,5120]{1,0:T(8,128)(2,1)}), bf16[256,5120]{1,0:T(8,128)(2,1)}) %all-gather.4.cloned.1.call-update) | async-done | bytes 2621456 | tf_op jit(solution)/shard_map/all_gather | solution.py:79
  71.1 5.4 %fusion.34 = f32[256,5120]{1,0:T(8,128)} fusion(f32[16,5120]{1,0:T(8,128)S(1)} %copy-done.5, bf16[256,5120]{1,0:T(8,128)(2,1)S(1)} %copy-done.3, f32[5120]{0:T(1024)S(1)} %bitcast.72, f32[256]{0:T(256)S(1)} %add_rsqrt_fusion.1, f32[16,5120]{1,0:T(8,128)S(1)} %copy-done.10), kind=kOutput, calls=%fused_computation.68 | convolution fusion | flops 89313280 | bytes 8541184 | tf_op jit(solution)/shard_map/dot_general | solution.py:87
  78.2 2.8 fusion.32
  81.8 8.5 %all-to-all-start.2 = ((f32[16,40,128]{2,1,0:T(8,128)}), f32[16,40,128]{2,1,0:T(8,128)S(1)}, u32[]{:S(2)}, u32[]{:S(2)}) async-start(f32[16,40,128]{2,1,0:T(8,128)} %bitcast.70), calls=%async_computation.4 | async-start | bytes 655360 | tf_op jit(solution)/shard_map/all_to_all | solution.py:128
  92.1 10.0 %all-to-all-done.2 = f32[16,40,128]{2,1,0:T(8,128)S(1)} async-done(((f32[16,40,128]{2,1,0:T(8,128)}), f32[16,40,128]{2,1,0:T(8,128)S(1)}, u32[]{:S(2)}, u32[]{:S(2)}) %all-to-all-start.2) | async-done | bytes 327712 | tf_op jit(solution)/shard_map/all_to_all | solution.py:128
  102.2 4.7 %all-to-all-start.6 = ((f32[16,40,128]{2,1,0:T(8,128)}), f32[16,40,128]{2,1,0:T(8,128)}, u32[]{:S(2)}, u32[]{:S(2)}) async-start(f32[16,40,128]{2,1,0:T(8,128)} %bitcast.69), calls=%async_computation.8 | async-start | bytes 655360 | tf_op jit(solution)/shard_map/all_to_all | solution.py:130
  108.6 9.3 %all-to-all-done.6 = f32[16,40,128]{2,1,0:T(8,128)} async-done(((f32[16,40,128]{2,1,0:T(8,128)}), f32[16,40,128]{2,1,0:T(8,128)}, u32[]{:S(2)}, u32[]{:S(2)}) %all-to-all-start.6) | async-done | bytes 327712 | tf_op jit(solution)/shard_map/all_to_all | solution.py:130
  118.0 4.9 %all-to-all-start.10 = ((f32[16,40,128]{2,1,0:T(8,128)}), f32[16,40,128]{2,1,0:T(8,128)}, u32[]{:S(2)}, u32[]{:S(2)}) async-start(f32[16,40,128]{2,1,0:T(8,128)} %bitcast.65), calls=%async_computation.12 | async-start | bytes 655360 | tf_op jit(solution)/shard_map/all_to_all | solution.py:132
  126.1 7.6 %all-to-all-done.10 = f32[16,40,128]{2,1,0:T(8,128)} async-done(((f32[16,40,128]{2,1,0:T(8,128)}), f32[16,40,128]{2,1,0:T(8,128)}, u32[]{:S(2)}, u32[]{:S(2)}) %all-to-all-start.10) | async-done | bytes 327712 | tf_op jit(solution)/shard_map/all_to_all | solution.py:132
  133.7 4.9 %all-to-all-start.4 = ((f32[16,40,128]{2,1,0:T(8,128)}), f32[16,40,128]{2,1,0:T(8,128)S(1)}, u32[]{:S(2)}, u32[]{:S(2)}) async-start(f32[16,40,128]{2,1,0:T(8,128)} %bitcast.15), calls=%async_computation.6 | async-start | bytes 655360 | tf_op jit(solution)/shard_map/all_to_all | solution.py:129
  140.6 8.5 %all-to-all-done.4 = f32[16,40,128]{2,1,0:T(8,128)S(1)} async-done(((f32[16,40,128]{2,1,0:T(8,128)}), f32[16,40,128]{2,1,0:T(8,128)S(1)}, u32[]{:S(2)}, u32[]{:S(2)}) %all-to-all-start.4) | async-done | bytes 327712 | tf_op jit(solution)/shard_map/all_to_all | solution.py:129
  149.1 4.9 %all-to-all-start.8 = ((f32[16,40,128]{2,1,0:T(8,128)}), f32[16,40,128]{2,1,0:T(8,128)S(1)}, u32[]{:S(2)}, u32[]{:S(2)}) async-start(f32[16,40,128]{2,1,0:T(8,128)} %bitcast.23), calls=%async_computation.10 | async-start | bytes 655360 | tf_op jit(solution)/shard_map/all_to_all | solution.py:131
  154.9 9.5 %all-to-all-done.8 = f32[16,40,128]{2,1,0:T(8,128)S(1)} async-done(((f32[16,40,128]{2,1,0:T(8,128)}), f32[16,40,128]{2,1,0:T(8,128)S(1)}, u32[]{:S(2)}, u32[]{:S(2)}) %all-to-all-start.8) | async-done | bytes 327712 | tf_op jit(solution)/shard_map/all_to_all | solution.py:131
  164.4 4.8 %all-to-all-start.12 = ((f32[16,40,128]{2,1,0:T(8,128)}), f32[16,40,128]{2,1,0:T(8,128)S(1)}, u32[]{:S(2)}, u32[]{:S(2)}) async-start(f32[16,40,128]{2,1,0:T(8,128)} %bitcast.31), calls=%async_computation.14 | async-start | bytes 655360 | tf_op jit(solution)/shard_map/all_to_all | solution.py:133
  181.0 2.9 fusion.23
  184.0 5.6 %all-to-all-start.13 = ((f32[16,40,128]{2,1,0:T(8,128)}), f32[16,40,128]{2,1,0:T(8,128)S(1)}, u32[]{:S(2)}, u32[]{:S(2)}) async-start(f32[16,40,128]{2,1,0:T(8,128)} %get-tuple-element.22), calls=%async_computation.15 | async-start | bytes 655360 | tf_op jit(solution)/shard_map/all_to_all | solution.py:147
  194.4 3.6 gather_fusion.1
  198.0 3.6 select_select_fusion
  202.3 8.1 %all-to-all-start.1 = ((bf16[16,16,5120]{2,1,0:T(8,128)(2,1)}), bf16[16,16,5120]{2,1,0:T(8,128)(2,1)}, u32[]{:S(2)}, u32[]{:S(2)}) async-start(bf16[16,16,5120]{2,1,0:T(8,128)(2,1)} %bitcast.7), calls=%async_computation.3 | async-start | bytes 5242880 | tf_op jit(solution)/shard_map/all_to_all | solution.py:121
  213.1 3.6 gather_fusion
  218.8 48.9 %all-to-all-done.1 = bf16[16,16,5120]{2,1,0:T(8,128)(2,1)} async-done(((bf16[16,16,5120]{2,1,0:T(8,128)(2,1)}), bf16[16,16,5120]{2,1,0:T(8,128)(2,1)}, u32[]{:S(2)}, u32[]{:S(2)}) %all-to-all-start.1) | async-done | bytes 2621472 | tf_op jit(solution)/shard_map/all_to_all | solution.py:121
  267.7 67.1 %all_to_all.114 = bf16[16,16,5120]{2,1,0:T(8,128)(2,1)} all-to-all(bf16[16,16,5120]{2,1,0:T(8,128)(2,1)S(1)} %bitcast.61), channel_id=1, replica_groups=mesh['section'=8,'peer'=16,'shard'=2] {'peer'}, dimensions={0} | all-to-all | bytes 5242880 | tf_op jit(solution)/shard_map/all_to_all | solution.py:118
  334.8 5.2 %all-to-all-start.11 = ((f32[16,40,128]{2,1,0:T(8,128)}), f32[16,40,128]{2,1,0:T(8,128)}, u32[]{:S(2)}, u32[]{:S(2)}) async-start(f32[16,40,128]{2,1,0:T(8,128)} %get-tuple-element.26), calls=%async_computation.13 | async-start | bytes 655360 | tf_op jit(solution)/shard_map/all_to_all | solution.py:146
  342.7 6.7 %collective-permute-start = (bf16[256,5120]{1,0:T(8,128)(2,1)}, bf16[256,5120]{1,0:T(8,128)(2,1)}, u32[]{:S(2)}, u32[]{:S(2)}) collective-permute-start(bf16[256,5120]{1,0:T(8,128)(2,1)} %bitcast.62), channel_id=1, source_target_pairs={{0,32},{32,64},{64,96},{96,128},{128,160},{160,192},{192,224},{1,3... | collective-permute-start | bytes 7864328 | tf_op jit(solution)/shard_map/ppermute | solution.py:18
  350.5 59.0 %all_to_all.115 = f32[16,40,128]{2,1,0:T(8,128)} all-to-all(f32[16,40,128]{2,1,0:T(8,128)} %get-tuple-element.25), channel_id=1, replica_groups=mesh['section'=8,'peer'=16,'shard'=2] {'peer'}, dimensions={0} | all-to-all | bytes 655360 | tf_op jit(solution)/shard_map/all_to_all | solution.py:145
  409.6 16.4 %all_to_all.116 = f32[16,40,128]{2,1,0:T(8,128)} all-to-all(f32[16,40,128]{2,1,0:T(8,128)S(1)} %copy-done.8), channel_id=1, replica_groups=mesh['section'=8,'peer'=16,'shard'=2] {'peer'}, dimensions={0} | all-to-all | bytes 655360 | tf_op jit(solution)/shard_map/all_to_all | solution.py:144
  425.9 14.0 %all_to_all.117 = f32[16,40,128]{2,1,0:T(8,128)} all-to-all(f32[16,40,128]{2,1,0:T(8,128)S(1)} %get-tuple-element.23), channel_id=1, replica_groups=mesh['section'=8,'peer'=16,'shard'=2] {'peer'}, dimensions={0} | all-to-all | bytes 655360 | tf_op jit(solution)/shard_map/all_to_all | solution.py:143
  439.9 4.5 all-to-all-start.3
  454.6 3.4 copy.51
  (110 shorter events, 60.6 us)
Async XLA Ops:
  7.2 21.7 %all-gather.8.cloned.1.call-start = ((), (), s32[]{:S(2)}) async-start(), calls=%async_computation.19 | async-start | bytes 3932160 | tf_op jit(solution)/shard_map/all_gather | solution.py:80
  7.9 23.5 %copy-start.10 = (f32[16,5120]{1,0:T(8,128)S(1)}, f32[16,5120]{1,0:T(8,128)}, u32[]{:S(2)}) copy-start(f32[16,5120]{1,0:T(8,128)} %param.24) | copy-start | bytes 983044
  7.9 40.7 %all-gather.6.cloned.1.call-start = ((), (), s32[]{:S(2)}) async-start(), calls=%async_computation.18 | async-start | bytes 3932160 | tf_op jit(solution)/shard_map/all_gather | solution.py:81
  8.7 59.9 %all-gather.4.cloned.1.call-start = ((), (), s32[]{:S(2)}) async-start(), calls=%async_computation.16 | async-start | bytes 3932160 | tf_op jit(solution)/shard_map/all_gather | solution.py:79
  9.4 180.1 %reduce-scatter.5.cloned.1.call-start = ((), (), s32[]{:S(2)}) async-start(), calls=%async_computation.20 | async-start | bytes 7864320 | tf_op jit(solution)/shard_map/reduce_scatter | solution.py:97
  28.9 2.5 copy-start.6
  31.4 17.3 %copy-start.5 = (f32[16,5120]{1,0:T(8,128)S(1)}, f32[16,5120]{1,0:T(8,128)}, u32[]{:S(2)}) copy-start(f32[16,5120]{1,0:T(8,128)} %param.25) | copy-start | bytes 983044
  54.5 156.6 %reduce-scatter.3.cloned.1.call-start = ((), (), s32[]{:S(2)}) async-start(), calls=%async_computation.17 | async-start | bytes 7864320 | tf_op jit(solution)/shard_map/reduce_scatter | solution.py:86
  68.5 2.5 copy-start.3
  81.0 41.8 %copy-start.2 = (bf16[256,5120]{1,0:T(8,128)(2,1)S(1)}, bf16[256,5120]{1,0:T(8,128)(2,1)}, u32[]{:S(2)}) copy-start(bf16[256,5120]{1,0:T(8,128)(2,1)} %all-gather.6.cloned.1.call-done) | copy-start | bytes 7864324
  81.8 20.3 %all-to-all-start.2 = ((f32[16,40,128]{2,1,0:T(8,128)}), f32[16,40,128]{2,1,0:T(8,128)S(1)}, u32[]{:S(2)}, u32[]{:S(2)}) async-start(f32[16,40,128]{2,1,0:T(8,128)} %bitcast.70), calls=%async_computation.4 | async-start | bytes 655360 | tf_op jit(solution)/shard_map/all_to_all | solution.py:128
  102.2 15.8 %all-to-all-start.6 = ((f32[16,40,128]{2,1,0:T(8,128)}), f32[16,40,128]{2,1,0:T(8,128)}, u32[]{:S(2)}, u32[]{:S(2)}) async-start(f32[16,40,128]{2,1,0:T(8,128)} %bitcast.69), calls=%async_computation.8 | async-start | bytes 655360 | tf_op jit(solution)/shard_map/all_to_all | solution.py:130
  118.0 15.7 %all-to-all-start.10 = ((f32[16,40,128]{2,1,0:T(8,128)}), f32[16,40,128]{2,1,0:T(8,128)}, u32[]{:S(2)}, u32[]{:S(2)}) async-start(f32[16,40,128]{2,1,0:T(8,128)} %bitcast.65), calls=%async_computation.12 | async-start | bytes 655360 | tf_op jit(solution)/shard_map/all_to_all | solution.py:132
  122.9 15.7 %copy-start.15 = (s32[1,16]{1,0:T(1,128)S(1)}, s32[1,16]{1,0:T(1,128)}, u32[]{:S(2)}) copy-start(s32[1,16]{1,0:T(1,128)} %param.22) | copy-start | bytes 196
  122.9 31.1 %copy-start.17 = (s32[1,16]{1,0:T(1,128)S(1)}, s32[1,16]{1,0:T(1,128)}, u32[]{:S(2)}) copy-start(s32[1,16]{1,0:T(1,128)} %param.23) | copy-start | bytes 196
  125.3 28.8 %copy-start.9 = (f32[2,8,40,128]{3,1,2,0:T(8,128)S(1)}, f32[2,8,40,128]{3,1,2,0:T(8,128)}, u32[]{:S(2)}) copy-start(f32[2,8,40,128]{3,1,2,0:T(8,128)} %get-tuple-element.16) | copy-start | bytes 983044
  133.7 15.4 %all-to-all-start.4 = ((f32[16,40,128]{2,1,0:T(8,128)}), f32[16,40,128]{2,1,0:T(8,128)S(1)}, u32[]{:S(2)}, u32[]{:S(2)}) async-start(f32[16,40,128]{2,1,0:T(8,128)} %bitcast.15), calls=%async_computation.6 | async-start | bytes 655360 | tf_op jit(solution)/shard_map/all_to_all | solution.py:129
  149.1 15.4 %all-to-all-start.8 = ((f32[16,40,128]{2,1,0:T(8,128)}), f32[16,40,128]{2,1,0:T(8,128)S(1)}, u32[]{:S(2)}, u32[]{:S(2)}) async-start(f32[16,40,128]{2,1,0:T(8,128)} %bitcast.23), calls=%async_computation.10 | async-start | bytes 655360 | tf_op jit(solution)/shard_map/all_to_all | solution.py:131
  164.4 15.3 %all-to-all-start.12 = ((f32[16,40,128]{2,1,0:T(8,128)}), f32[16,40,128]{2,1,0:T(8,128)S(1)}, u32[]{:S(2)}, u32[]{:S(2)}) async-start(f32[16,40,128]{2,1,0:T(8,128)} %bitcast.31), calls=%async_computation.14 | async-start | bytes 655360 | tf_op jit(solution)/shard_map/all_to_all | solution.py:133
  181.0 8.5 %copy-start = (bf16[128,5120]{1,0:T(8,128)(2,1)S(1)}, bf16[128,5120]{1,0:T(8,128)(2,1)}, u32[]{:S(2)}) copy-start(bf16[128,5120]{1,0:T(8,128)(2,1)} %param.18) | copy-start | bytes 3932164
  184.0 17.6 %all-to-all-start.13 = ((f32[16,40,128]{2,1,0:T(8,128)}), f32[16,40,128]{2,1,0:T(8,128)S(1)}, u32[]{:S(2)}, u32[]{:S(2)}) async-start(f32[16,40,128]{2,1,0:T(8,128)} %get-tuple-element.22), calls=%async_computation.15 | async-start | bytes 655360 | tf_op jit(solution)/shard_map/all_to_all | solution.py:147
  189.6 2.5 copy-start.1
  201.6 8.9 %copy-start.16 = (s32[1,16]{1,0:T(1,128)S(1)}, s32[1,16]{1,0:T(1,128)}, u32[]{:S(2)}) copy-start(s32[1,16]{1,0:T(1,128)} %param.21) | copy-start | bytes 196
  201.6 9.5 %copy-start.4 = (bf16[128,5120]{1,0:T(8,128)(2,1)S(1)}, bf16[128,5120]{1,0:T(8,128)(2,1)}, u32[]{:S(2)}) copy-start(bf16[128,5120]{1,0:T(8,128)(2,1)} %param.17) | copy-start | bytes 3932164
  202.3 65.4 %all-to-all-start.1 = ((bf16[16,16,5120]{2,1,0:T(8,128)(2,1)}), bf16[16,16,5120]{2,1,0:T(8,128)(2,1)}, u32[]{:S(2)}, u32[]{:S(2)}) async-start(bf16[16,16,5120]{2,1,0:T(8,128)(2,1)} %bitcast.7), calls=%async_computation.3 | async-start | bytes 5242880 | tf_op jit(solution)/shard_map/all_to_all | solution.py:121
  267.7 141.9 %copy-start.8 = (f32[16,40,128]{2,1,0:T(8,128)S(1)}, f32[16,40,128]{2,1,0:T(8,128)}, u32[]{:S(2)}) copy-start(f32[16,40,128]{2,1,0:T(8,128)} %get-tuple-element.24) | copy-start | bytes 983044
  334.8 15.7 %all-to-all-start.11 = ((f32[16,40,128]{2,1,0:T(8,128)}), f32[16,40,128]{2,1,0:T(8,128)}, u32[]{:S(2)}, u32[]{:S(2)}) async-start(f32[16,40,128]{2,1,0:T(8,128)} %get-tuple-element.26), calls=%async_computation.13 | async-start | bytes 655360 | tf_op jit(solution)/shard_map/all_to_all | solution.py:146
  340.0 114.6 %collective-permute-start.1 = (bf16[256,5120]{1,0:T(8,128)(2,1)}, bf16[256,5120]{1,0:T(8,128)(2,1)S(1)}, u32[]{:S(2)}, u32[]{:S(2)}) collective-permute-start(bf16[256,5120]{1,0:T(8,128)(2,1)} %bitcast.8), channel_id=1, source_target_pairs={{32,0},{64,32},{96,64},{128,96},{160,128},{192,160},{224,192},{33,... | collective-permute-start | bytes 7864328 | tf_op jit(solution)/shard_map/ppermute | solution.py:18
  342.7 111.9 %collective-permute-start = (bf16[256,5120]{1,0:T(8,128)(2,1)}, bf16[256,5120]{1,0:T(8,128)(2,1)}, u32[]{:S(2)}, u32[]{:S(2)}) collective-permute-start(bf16[256,5120]{1,0:T(8,128)(2,1)} %bitcast.62), channel_id=1, source_target_pairs={{0,32},{32,64},{64,96},{96,128},{128,160},{160,192},{192,224},{1,3... | collective-permute-start | bytes 7864328 | tf_op jit(solution)/shard_map/ppermute | solution.py:18
  425.9 22.0 %copy-start.12 = (f32[16,40,128]{2,1,0:T(8,128)S(1)}, f32[16,40,128]{2,1,0:T(8,128)}, u32[]{:S(2)}) copy-start(f32[16,40,128]{2,1,0:T(8,128)} %all_to_all.115) | copy-start | bytes 983044
  439.9 13.9 %all-to-all-start.3 = ((f32[16,40,128]{2,1,0:T(8,128)}), f32[16,40,128]{2,1,0:T(8,128)S(1)}, u32[]{:S(2)}, u32[]{:S(2)}) async-start(f32[16,40,128]{2,1,0:T(8,128)} %get-tuple-element.27), calls=%async_computation.5 | async-start | bytes 655360 | tf_op jit(solution)/shard_map/all_to_all | solution.py:142
  444.4 6.1 %copy-start.13 = (f32[16,40,128]{2,1,0:T(8,128)S(1)}, f32[16,40,128]{2,1,0:T(8,128)}, u32[]{:S(2)}) copy-start(f32[16,40,128]{2,1,0:T(8,128)} %all_to_all.117) | copy-start | bytes 983044
  (3 other events, 4.8 us)
Sparse Core Ops, SparseCore 0:
  9.8 19.0 all-gather.7
  30.7 17.9 all-gather.5
  50.5 18.0 all-gather.3
  70.9 19.8 reduce-scatter.4
  93.4 19.8 reduce-scatter.2
where the time goes:
time: 468 us; the launch traced here: 466 us
  blocking collectives  156 us (33%)
  waiting for transfers between devices  152 us (32%)
  starting transfers between devices  65.7 us (14%)
  local copies, waits for them, and re-layouts  39.4 us (8%)
  other arithmetic  21.2 us (5%)
  matrix products  17.3 us (4%)
  between operations  14 us (3%)
    all_to_all x1, blocking collectives, local(): lax.all_to_all(packed_out, 'peer', split_axis=0, concat_axis=0, tiled=True)  67.1 us
    all_to_all x1, blocking collectives, local(): lax.all_to_all(averaged[3], 'peer', split_axis=0, concat_axis=0, tiled=True)  59 us
    all_to_all x1, waiting for transfers between devices, local(): lax.all_to_all(packed_grad, 'peer', split_axis=0, concat_axis=0, tiled=True)  48.9 us
    unnamed x50, local copies, waits for them, and re-layouts  22.8 us
    all_gather x1, waiting for transfers between devices, local(): lax.all_gather(saved_rows, 'shard', axis=0, tiled=True)  19.4 us
    all_gather x1, waiting for transfers between devices, local(): lax.all_gather(output_grad, 'shard', axis=0, tiled=True)  16.4 us
    all_to_all x1, blocking collectives, local(): lax.all_to_all(averaged[2], 'peer', split_axis=0, concat_axis=0, tiled=True)  16.4 us
    all_gather x1, waiting for transfers between devices, local(): lax.all_gather(forward_rows, 'shard', axis=0, tiled=True)  14 us
  transfers between devices with their start and end apart: 17, of which 12 were waited for; matrix products, arithmetic and copies ran while one was open for 15% of the time, Pallas kernels for 0%

commit v1 on v0

v1 whole, which is shorter than its diff:
```python
import functools

import jax
import jax.numpy as jnp
from jax import lax
from jax.experimental import pallas as pl
from jax.experimental.pallas import tpu as pltpu
from jax.sharding import PartitionSpec as P

MESH = pl.DeviceIdType.MESH
AXES = ("section", "peer", "shard")
LANE = 128
WIDE = 512
beta_one = 0.9
beta_two = 0.999
learn_rate = 0.001
adam_eps = 1e-08
norm_eps = 1e-05
step_count = 20
F32 = jnp.float32
BF16 = jnp.bfloat16


def dot_nt(a, b):
    return lax.dot_general(a, b, (((1,), (1,)), ((), ())), preferred_element_type=F32)


def dot_nn(a, b):
    return jnp.dot(a, b, preferred_element_type=F32)


def sigmoid(v):
    return 1.0 / (1.0 + jnp.exp(-v))


def kernel(
    sections,
    peers,
    near,
    x_hbm,
    y_hbm,
    g_hbm,
    gain_hbm,
    fcnt,
    rcnt,
    mat,
    dw_hbm,
    uw_hbm,
    dm_hbm,
    um_hbm,
    dv_hbm,
    uv_hbm,
    arrived,
    returned,
    o_dw,
    o_uw,
    o_dm,
    o_um,
    o_dv,
    o_uv,
    x_v,
    y_v,
    g_v,
    gain_v,
    st,
    wown,
    woth,
    pk_f,
    pk_b,
    ns,
    hot_f,
    hot_b,
    part_own,
    part_out,
    part_in,
    gs1,
    gr1,
    gs2,
    gr2,
    zero,
    in_sem,
    w_send,
    w_recv,
    p_send,
    p_recv,
    f_send,
    f_recv,
    b_send,
    b_recv,
    g1_send,
    g1_recv,
    g2_send,
    g2_recv,
    out_sem,
):
    s = lax.axis_index("section")
    p = lax.axis_index("peer")
    c = lax.axis_index("shard")
    rows, depth = x_v.shape
    unit = st.shape[1]
    cap = zero.shape[0]
    steps = depth // WIDE
    blocks = depth // LANE
    has_next = s < sections - 1
    has_prev = s > 0
    nxt = s + 1
    prv = s - 1

    def peer_at(k):
        z = lax.rem(lax.rem(p, near) + lax.rem(k, near), near)
        x = lax.rem(p // near + k // near, peers // near)
        return x * near + z

    state_hbm = (dw_hbm, uw_hbm, dm_hbm, um_hbm, dv_hbm, uv_hbm)
    outs = (o_dw, o_uw, o_dm, o_um, o_dv, o_uv)
    loads = [
        pltpu.make_async_copy(dw_hbm, st.at[0], in_sem.at[0]),
        pltpu.make_async_copy(uw_hbm, st.at[1], in_sem.at[1]),
        pltpu.make_async_copy(gain_hbm, gain_v, in_sem.at[2]),
        pltpu.make_async_copy(x_hbm, x_v, in_sem.at[3]),
        pltpu.make_async_copy(y_hbm, y_v, in_sem.at[4]),
        pltpu.make_async_copy(g_hbm, g_v, in_sem.at[5]),
    ] + [pltpu.make_async_copy(state_hbm[i], st.at[i], in_sem.at[4 + i]) for i in range(2, 6)]
    for load in loads:
        load.start()

    barrier = pltpu.get_barrier_semaphore()

    def greet(k, carry):
        q = peer_at(k)

        @pl.when(has_next)
        def _():
            pl.semaphore_signal(barrier, inc=1, device_id=(nxt, q, c), device_id_type=MESH)

        @pl.when(has_prev)
        def _():
            pl.semaphore_signal(barrier, inc=1, device_id=(prv, q, c), device_id_type=MESH)

        @pl.when(k > 0)
        def _():
            pl.semaphore_signal(barrier, inc=1, device_id=(s, q, c), device_id_type=MESH)

        return carry

    pl.semaphore_signal(barrier, inc=1, device_id=(s, p, 1 - c), device_id_type=MESH)
    lax.fori_loop(0, peers, greet, 0)

    zero[...] = jnp.zeros_like(zero)

    row_id = lax.broadcasted_iota(jnp.int32, (cap, rows), 0)
    col_id = lax.broadcasted_iota(jnp.int32, (cap, rows), 1)
    for cnt, hot in ((fcnt, hot_f), (rcnt, hot_b)):
        offset = jnp.int32(0)
        for q in range(peers):
            n = cnt[0, q]
            pick = (col_id == offset + row_id) & (row_id < n)
            hot[pl.ds(q * cap, cap), :] = jnp.where(pick, 1.0, 0.0).astype(BF16)
            offset = offset + n

    loads[0].wait()
    loads[1].wait()
    for i in range(2):
        for j in range(steps):
            wown[i, :, pl.ds(j * WIDE, WIDE)] = st[i, :, pl.ds(j * WIDE, WIDE)].astype(BF16)

    groups = 1 + jnp.where(has_next, 1, 0) + jnp.where(has_prev, 1, 0)
    pl.semaphore_wait(barrier, peers * groups)

    w_copy = pltpu.make_async_remote_copy(
        src_ref=wown,
        dst_ref=woth,
        send_sem=w_send,
        recv_sem=w_recv,
        device_id=(s, p, 1 - c),
        device_id_type=MESH,
    )
    w_copy.start()

    def inverse(ref):
        def body(j, acc):
            for t in range(WIDE // LANE):
                v = ref[:, pl.ds(pl.multiple_of(j * WIDE + t * LANE, LANE), LANE)].astype(F32)
                acc = acc + v * v
            return acc

        acc = lax.fori_loop(0, steps, body, jnp.zeros((rows, LANE), F32))
        return 1.0 / jnp.sqrt(jnp.sum(acc, axis=-1, keepdims=True) / depth + norm_eps)

    def cols(j):
        return pl.ds(pl.multiple_of(j * WIDE, WIDE), WIDE)

    loads[2].wait()
    loads[3].wait()
    r_f = inverse(x_v)

    def norm_f(j, carry):
        v = x_v[:, cols(j)].astype(F32) * r_f * gain_v[:, cols(j)].astype(F32)
        ns[:, cols(j)] = v.astype(BF16)
        return carry

    lax.fori_loop(0, steps, norm_f, 0)
    w_copy.wait()

    def pre_of(j, carry):
        own, oth = carry
        v = ns[:, cols(j)]
        return own + dot_nt(v, wown[0, :, cols(j)]), oth + dot_nt(v, woth[0, :, cols(j)])

    blank = jnp.zeros((rows, unit), F32)
    pre_own, pre_oth = lax.fori_loop(0, steps, pre_of, (blank, blank))
    act_own = (pre_own * sigmoid(pre_own)).astype(BF16)
    act_oth = (pre_oth * sigmoid(pre_oth)).astype(BF16)

    def out_f(j, carry):
        up = jnp.concatenate([wown[1, :, cols(j)], woth[1, :, cols(j)]], axis=0)
        act = jnp.concatenate([act_own, act_oth], axis=1)
        v = (x_v[:, cols(j)].astype(F32) + dot_nn(act, up)).astype(BF16)
        pk_f[:, cols(j)] = dot_nn(hot_f[...], v).astype(BF16)
        return carry

    lax.fori_loop(0, steps, out_f, 0)

    def route(k, pk, out, target, send, recv):
        q = peer_at(k)
        return pltpu.make_async_remote_copy(
            src_ref=pk.at[pl.ds(pl.multiple_of(q * cap, cap), cap)],
            dst_ref=out.at[pl.ds(pl.multiple_of(p * cap, cap), cap)],
            send_sem=send.at[k],
            recv_sem=recv.at[p],
            device_id=(target, q, c),
            device_id_type=MESH,
        )

    @pl.when(has_next)
    def _():
        def go(k, carry):
            route(k, pk_f, arrived, nxt, f_send, f_recv).start()
            return carry

        lax.fori_loop(0, peers, go, 0)

    loads[4].wait()
    r_s = inverse(y_v)

    def norm_s(j, carry):
        v = y_v[:, cols(j)].astype(F32) * r_s * gain_v[:, cols(j)].astype(F32)
        ns[:, cols(j)] = v.astype(BF16)
        return carry

    lax.fori_loop(0, steps, norm_s, 0)
    loads[5].wait()

    def pre_s_of(j, carry):
        a, b, d, e = carry
        v = ns[:, cols(j)]
        g = g_v[:, cols(j)]
        return (
            a + dot_nt(v, wown[0, :, cols(j)]),
            b + dot_nt(v, woth[0, :, cols(j)]),
            d + dot_nt(g, wown[1, :, cols(j)]),
            e + dot_nt(g, woth[1, :, cols(j)]),
        )

    s_own, s_oth, ga_own, ga_oth = lax.fori_loop(0, steps, pre_s_of, (blank, blank, blank, blank))

    pre_s = jnp.concatenate([s_own, s_oth], axis=1)
    grad_act = jnp.concatenate([ga_own, ga_oth], axis=1)
    sig = sigmoid(pre_s)
    act_s = (pre_s * sig).astype(BF16)
    grad_pre = (grad_act * (sig * (1.0 + pre_s * (1.0 - sig)))).astype(BF16)
    inner = jnp.sum(grad_pre.astype(F32) * pre_s, axis=-1, keepdims=True)
    pull = inner * r_s * r_s / depth

    def grads(j, carry):
        g = g_v[:, cols(j)]
        gu = lax.dot_general(act_s, g, (((0,), (0,)), ((), ())), preferred_element_type=F32)
        gd = lax.dot_general(
            grad_pre, ns[:, cols(j)], (((0,), (0,)), ((), ())), preferred_element_type=F32
        )
        part_own[0, :, cols(j)] = gd[:unit]
        part_out[0, :, cols(j)] = gd[unit:]
        part_own[1, :, cols(j)] = gu[:unit]
        part_out[1, :, cols(j)] = gu[unit:]
        return carry

    lax.fori_loop(0, steps, grads, 0)
    p_copy = pltpu.make_async_remote_copy(
        src_ref=part_out,
        dst_ref=part_in,
        send_sem=p_send,
        recv_sem=p_recv,
        device_id=(s, p, 1 - c),
        device_id_type=MESH,
    )
    p_copy.start()

    def out_b(j, carry):
        down = jnp.concatenate([wown[0, :, cols(j)], woth[0, :, cols(j)]], axis=0)
        u = dot_nn(grad_pre, down) * gain_v[:, cols(j)].astype(F32)
        y = y_v[:, cols(j)].astype(F32)
        v = (g_v[:, cols(j)].astype(F32) + u * r_s - y * pull).astype(BF16)
        pk_b[:, cols(j)] = dot_nn(hot_b[...], v).astype(BF16)
        return carry

    lax.fori_loop(0, steps, out_b, 0)

    for i in range(6, 10):
        loads[i].wait()
    p_copy.wait()

    first_fix = 1.0 - beta_one**step_count
    second_fix = 1.0 - beta_two**step_count

    def tile(a, j):
        return pl.ds(pl.multiple_of((a * blocks + j) * unit, unit), unit)

    def adam(j, carry):
        at = pl.ds(pl.multiple_of(j * LANE, LANE), LANE)
        for i in range(2):
            grad = part_own[i, :, at] + part_in[i, :, at]
            m = beta_one * st[2 + i, :, at] + (1.0 - beta_one) * grad
            v = beta_two * st[4 + i, :, at] + (1.0 - beta_two) * grad * grad
            w = st[i, :, at] - learn_rate * (m / first_fix) / (
                jnp.sqrt(v / second_fix) + adam_eps
            )
            for a, value in ((i, w), (2 + i, m), (4 + i, v)):
                st[a, :, at] = value
                gs1[tile(a, j), :] = value.astype(BF16)
        return carry

    lax.fori_loop(0, blocks, adam, 0)

    piece = gr1.shape[1]

    def slab(q):
        return pl.ds(pl.multiple_of(q * piece, piece), piece)

    def gossip(k, src, dst, send, recv):
        q = peer_at(k)
        return pltpu.make_async_remote_copy(
            src_ref=src(q),
            dst_ref=dst.at[p],
            send_sem=send.at[k],
            recv_sem=recv.at[p],
            device_id=(s, q, c),
            device_id_type=MESH,
        )

    def one(q):
        return gs1.at[slab(q)]

    def two(q):
        return gs2.at[q]

    def go_one(k, carry):
        gossip(k, one, gr1, g1_send, g1_recv).start()
        return carry

    lax.fori_loop(1, peers, go_one, 0)
    gr1[p] = gs1[slab(p), :]

    @pl.when(has_prev)
    def _():
        def go(k, carry):
            route(k, pk_b, returned, prv, b_send, b_recv).start()
            return carry

        lax.fori_loop(0, peers, go, 0)

    @pl.when(s == 0)
    def _():
        for q in range(peers):
            pltpu.make_async_copy(zero, arrived.at[pl.ds(q * cap, cap)], f_recv.at[q]).start()

    @pl.when(s == sections - 1)
    def _():
        for q in range(peers):
            pltpu.make_async_copy(zero, returned.at[pl.ds(q * cap, cap)], b_recv.at[q]).start()

    def wait_one(k, carry):
        q = peer_at(k)
        pltpu.make_async_copy(gr1.at[q], gr1.at[q], g1_recv.at[q]).wait()
        return carry

    lax.fori_loop(1, peers, wait_one, 0)

    def swap(q, carry):
        m = mat[0, q]
        gs2[q] = gr1[m]
        return carry

    lax.fori_loop(0, peers, swap, 0)

    def go_two(k, carry):
        gossip(k, two, gr2, g2_send, g2_recv).start()
        return carry

    lax.fori_loop(1, peers, go_two, 0)
    gr2[p] = gs2[p]

    def wait_two(k, carry):
        q = peer_at(k)
        pltpu.make_async_copy(gr2.at[q], gr2.at[q], g2_recv.at[q]).wait()
        return carry

    lax.fori_loop(1, peers, wait_two, 0)

    per = piece // unit

    def average(j, carry):
        at = pl.ds(pl.multiple_of(j * LANE, LANE), LANE)
        for a in range(6):
            t = a * blocks + j
            k = lax.rem(t, per)
            value = gr2[lax.div(t, per), pl.ds(pl.multiple_of(k * unit, unit), unit), :]
            st[a, :, at] = (st[a, :, at] + value.astype(F32)) * 0.5
        return carry

    lax.fori_loop(0, blocks, average, 0)
    stores = [pltpu.make_async_copy(st.at[a], outs[a], out_sem.at[a]) for a in range(6)]
    for store in stores:
        store.start()

    def finish(k, carry):
        pltpu.make_async_copy(
            arrived.at[pl.ds(k * cap, cap)], arrived.at[pl.ds(k * cap, cap)], f_recv.at[k]
        ).wait()
        pltpu.make_async_copy(
            returned.at[pl.ds(k * cap, cap)], returned.at[pl.ds(k * cap, cap)], b_recv.at[k]
        ).wait()

        @pl.when(has_next)
        def _():
            route(k, pk_f, arrived, nxt, f_send, f_recv).wait_send()

        @pl.when(has_prev)
        def _():
            route(k, pk_b, returned, prv, b_send, b_recv).wait_send()

        @pl.when(k > 0)
        def _():
            gossip(k, one, gr1, g1_send, g1_recv).wait_send()
            gossip(k, two, gr2, g2_send, g2_recv).wait_send()

        return carry

    lax.fori_loop(0, peers, finish, 0)
    for store in stores:
        store.wait()


def local(sections, peers, near, *args):
    rows, depth = args[0].shape
    unit = args[7].shape[0]
    cap = 2 * rows // peers
    slots = peers * cap
    flat = 6 * unit * depth // LANE
    any_spec = pl.BlockSpec(memory_space=pl.ANY)
    smem = pl.BlockSpec(memory_space=pltpu.SMEM)
    dma = pltpu.SemaphoreType.DMA
    return pl.pallas_call(
        functools.partial(kernel, sections, peers, near),
        out_shape=[jax.ShapeDtypeStruct((slots, depth), BF16)] * 2
        + [jax.ShapeDtypeStruct((unit, depth), F32)] * 6,
        in_specs=[any_spec] * 4 + [smem] * 3 + [any_spec] * 6,
        out_specs=[any_spec] * 8,
        scratch_shapes=[
            pltpu.VMEM((rows, depth), BF16),
            pltpu.VMEM((rows, depth), BF16),
            pltpu.VMEM((rows, depth), BF16),
            pltpu.VMEM((1, depth), BF16),
            pltpu.VMEM((6, unit, depth), F32),
            pltpu.VMEM((2, unit, depth), BF16),
            pltpu.VMEM((2, unit, depth), BF16),
            pltpu.VMEM((slots, depth), BF16),
            pltpu.VMEM((slots, depth), BF16),
            pltpu.VMEM((rows, depth), BF16),
            pltpu.VMEM((slots, rows), BF16),
            pltpu.VMEM((slots, rows), BF16),
            pltpu.VMEM((2, unit, depth), F32),
            pltpu.VMEM((2, unit, depth), F32),
            pltpu.VMEM((2, unit, depth), F32),
            pltpu.VMEM((flat, LANE), BF16),
            pltpu.VMEM((peers, flat // peers, LANE), BF16),
            pltpu.VMEM((peers, flat // peers, LANE), BF16),
            pltpu.VMEM((peers, flat // peers, LANE), BF16),
            pltpu.VMEM((cap, depth), BF16),
            dma((10,)),
            dma,
            dma,
            dma,
            dma,
            dma((peers,)),
            dma((peers,)),
            dma((peers,)),
            dma((peers,)),
            dma((peers,)),
            dma((peers,)),
            dma((peers,)),
            dma((peers,)),
            dma((6,)),
        ],
        compiler_params=pltpu.CompilerParams(
            collective_id=0, has_side_effects=True, vmem_limit_bytes=48 * 2**20
        ),
    )(*args)


def solution(mesh):
    sections, peers = mesh.shape["section"], mesh.shape["peer"]
    rows = P(AXES, None)
    by_section = P("section", None)
    return jax.shard_map(
        functools.partial(local, sections, peers, peers // 2),
        mesh=mesh,
        in_specs=(rows, rows, rows, by_section, rows, rows, by_section) + (rows,) * 6,
        out_specs=(rows,) * 8,
        check_vma=False,
    )
```

time: 468 us -> 225 us (0.48)
  the two profiles are of different devices: /device:TPU:56 before, /device:TPU:140 now
where the time goes in v1:
time: 225 us
  Pallas kernels  205 us (91%)
  local copies, waits for them, and re-layouts  19.2 us (9%)
    pallas_call x1, Pallas kernels, local(): pl.pallas_call(functools.partial(kernel, sections, peers, near), out_shap...  205 us
    unnamed x32, local copies, waits for them, and re-layouts  19.2 us

profile of v1, /device:TPU:140, one launch (start us, length us, event | category | flops | bytes accessed | tf_op | source)
XLA Modules:
  0.0 225.0 jit_solution(15172263193773975037)
XLA Ops:
  0.6 0.0 copy-start
  0.6 1.3 copy-done
  2.0 0.0 copy-start.1
  2.0 1.0 copy-done.1
  2.9 0.0 copy-start.2
  2.9 1.0 copy-done.2
  3.9 0.0 copy-start.3
  3.9 1.0 copy-done.3
  4.9 0.0 copy-start.4
  4.9 1.0 copy-done.4
  5.8 0.0 copy-start.5
  5.9 1.0 copy-done.5
  6.8 0.0 copy-start.6
  6.8 1.0 copy-done.6
  7.8 0.0 copy-start.7
  7.8 0.7 copy-done.7
  8.5 0.0 copy-start.8
  8.5 0.7 copy-done.8
  9.2 0.0 copy-start.9
  9.2 0.7 copy-done.9
  9.8 0.7 copy-done.10
  10.5 205.1 %shard_map.188 = (bf16[256,5120]{1,0:T(8,128)(2,1)}, bf16[256,5120]{1,0:T(8,128)(2,1)}, f32[16,5120]{1,0:T(8,128)S(1)}, f32[16,5120]{1,0:T(8,128)S(1)}, f32[16,5...) custom-call(bf16[128,5120]{1,0:T(8,128)(2,1)S(1)} %copy-done, ...), custom_call_target="tpu_custom_call" | custom-call | tf_op jit(solution)/shard_map/pallas_call | solution.py:462
  215.6 0.0 copy-start.11
  215.6 3.6 %copy.29 = bf16[256,5120]{1,0:T(8,128)(2,1)} copy(bf16[256,5120]{1,0:T(8,128)(2,1)} %get-tuple-element.16) | data formatting | bytes 5242880
  219.2 0.0 copy-done.11
  219.2 1.5 copy.30
  220.7 0.7 copy.31
  221.4 0.7 copy.32
  222.1 0.7 copy.33
  222.9 0.7 copy.34
  223.6 0.7 copy.35
  224.3 0.7 copy.36
  (1 shorter events, 0.0 us)
Async XLA Ops:
  0.6 1.3 copy-start
  2.0 1.0 copy-start.1
  2.9 1.0 copy-start.2
  3.9 1.0 copy-start.3
  4.9 1.0 copy-start.4
  5.8 1.0 copy-start.5
  6.8 1.0 copy-start.6
  7.8 0.7 copy-start.7
  8.5 0.7 copy-start.8
  9.2 0.7 copy-start.9
  9.8 0.7 copy-start.10
  215.6 3.6 %copy-start.11 = (bf16[256,5120]{1,0:T(8,128)(2,1)S(1)}, bf16[256,5120]{1,0:T(8,128)(2,1)}, u32[]{:S(2)}) copy-start(bf16[256,5120]{1,0:T(8,128)(2,1)} %get-tuple-element.17) | copy-start | bytes 7864324

commit v2 on v1

v2 whole, which is shorter than its diff:
```python
import functools

import jax
import jax.numpy as jnp
from jax import lax
from jax.experimental import pallas as pl
from jax.experimental.pallas import tpu as pltpu
from jax.sharding import PartitionSpec as P

MESH = pl.DeviceIdType.MESH
AXES = ("section", "peer", "shard")
LANE = 128
WIDE = 512
CHUNKS = 4
RELAYS = 3
beta_one = 0.9
beta_two = 0.999
learn_rate = 0.001
adam_eps = 1e-08
norm_eps = 1e-05
step_count = 20
first_fix = 1.0 - beta_one**step_count
second_fix = 1.0 - beta_two**step_count
F32 = jnp.float32
BF16 = jnp.bfloat16


def dot_nt(a, b):
    return lax.dot_general(a, b, (((1,), (1,)), ((), ())), preferred_element_type=F32)


def dot_tn(a, b):
    return lax.dot_general(a, b, (((0,), (0,)), ((), ())), preferred_element_type=F32)


def dot_nn(a, b):
    return jnp.dot(a, b, preferred_element_type=F32)


def sigmoid(v):
    return 1.0 / (1.0 + jnp.exp(-v))


def stepped(weight, moment, second):
    return weight - learn_rate * (moment / first_fix) / (
        jnp.sqrt(second / second_fix) + adam_eps
    )


def arrived_all(ref, sem):
    pltpu.make_async_copy(ref, ref, sem).wait()


def kernel(
    sections,
    peers,
    near,
    x_hbm,
    y_hbm,
    g_hbm,
    gain_hbm,
    fcnt,
    rcnt,
    mat,
    dw_hbm,
    uw_hbm,
    dm_hbm,
    um_hbm,
    dv_hbm,
    uv_hbm,
    arrived,
    returned,
    o_dw,
    o_uw,
    o_dm,
    o_um,
    o_dv,
    o_uv,
    xu,
    wdn,
    y_v,
    g_v,
    gain_v,
    st,
    scaled,
    pk_f,
    pk_b,
    hot_f,
    hot_b,
    part_own,
    part_out,
    part_in,
    w1s,
    w1r,
    w2s,
    w2r,
    m1s,
    m1r,
    m2s,
    m2r,
    relay,
    zero,
    in_sem,
    w_send,
    w_recv,
    p_send,
    p_recv,
    f_send,
    f_recv,
    b_send,
    b_recv,
    q_send,
    q_recv,
    l_send,
    gw_sem,
    gm_sem,
    out_sem,
):
    s = lax.axis_index("section")
    p = lax.axis_index("peer")
    c = lax.axis_index("shard")
    rows, depth = y_v.shape
    unit = st.shape[1]
    cap = 2 * rows // peers
    steps = depth // WIDE
    blocks = depth // LANE
    part = depth // CHUNKS
    has_next = s < sections - 1
    has_prev = s > 0
    nxt = s + 1
    prv = s - 1
    half = sections // 2
    out_f_relays = jnp.where(has_next, jnp.maximum(s - (half - 1), 0), 0)
    out_b_relays = jnp.where(has_prev, jnp.maximum(half - s, 0), 0)
    in_f_relays = jnp.maximum(s - half, 0)
    in_b_relays = jnp.maximum(half - 1 - s, 0)

    px = p // near
    pz = lax.rem(p, near)

    def peer_at(k):
        j = k // 2
        h = (j + 1) // 2
        dz = (near // 2 - h) * (2 * lax.rem(j, 2) - 1)
        x = lax.rem(px + 1 - lax.rem(k, 2), 2)
        return x * near + lax.rem(pz + dz + near, near)

    others = peers - 1

    state_hbm = (dw_hbm, uw_hbm, dm_hbm, um_hbm, dv_hbm, uv_hbm)
    outs = (o_dw, o_uw, o_dm, o_um, o_dv, o_uv)
    loads = [
        pltpu.make_async_copy(dw_hbm, st.at[0], in_sem.at[0]),
        pltpu.make_async_copy(uw_hbm, st.at[1], in_sem.at[1]),
        pltpu.make_async_copy(gain_hbm, gain_v, in_sem.at[2]),
        pltpu.make_async_copy(x_hbm, xu.at[pl.ds(0, rows)], in_sem.at[3]),
        pltpu.make_async_copy(y_hbm, y_v, in_sem.at[4]),
        pltpu.make_async_copy(g_hbm, g_v, in_sem.at[5]),
    ] + [pltpu.make_async_copy(state_hbm[i], st.at[i], in_sem.at[4 + i]) for i in range(2, 6)]
    for load in loads:
        load.start()

    barrier = pltpu.get_barrier_semaphore()

    def greet(k, carry):
        q = peer_at(k)

        @pl.when(has_next)
        def _():
            pl.semaphore_signal(barrier, inc=1, device_id=(nxt, q, c), device_id_type=MESH)

        @pl.when(has_prev)
        def _():
            pl.semaphore_signal(barrier, inc=1, device_id=(prv, q, c), device_id_type=MESH)

        @pl.when(k < others)
        def _():
            pl.semaphore_signal(barrier, inc=1, device_id=(s, q, c), device_id_type=MESH)

        return carry

    pl.semaphore_signal(barrier, inc=1, device_id=(s, p, 1 - c), device_id_type=MESH)
    lax.fori_loop(0, peers, greet, 0)

    def tile(a, j):
        return pl.ds(pl.multiple_of((a * blocks + j) * unit, unit), unit)

    def lanes(j):
        return pl.ds(pl.multiple_of(j * LANE, LANE), LANE)

    loads[0].wait()
    loads[1].wait()

    def cast(j, carry):
        down = st[0, :, lanes(j)].astype(BF16)
        up = st[1, :, lanes(j)].astype(BF16)
        wdn[pl.ds(0, unit), lanes(j)] = down
        xu[pl.ds(rows, unit), lanes(j)] = up
        w1s[tile(0, j), :] = down
        w1s[tile(1, j), :] = up
        return carry

    lax.fori_loop(0, blocks, cast, 0)

    row_id = lax.broadcasted_iota(jnp.int32, (cap, rows), 0)
    col_id = lax.broadcasted_iota(jnp.int32, (cap, rows), 1)

    def slot_matrix(cnt, hot):
        offset = jnp.int32(0)
        for q in range(peers):
            n = cnt[0, q]
            pick = (col_id == offset + row_id) & (row_id < n)
            hot[pl.ds(q * cap, cap), :] = jnp.where(pick, 1.0, 0.0).astype(BF16)
            offset = offset + n

    slot_matrix(fcnt, hot_f)

    groups = 1 + jnp.where(has_next, 1, 0) + jnp.where(has_prev, 1, 0)
    pl.semaphore_wait(barrier, peers * groups)

    partner = (s, p, 1 - c)
    w_copies = [
        pltpu.make_async_remote_copy(
            src_ref=wdn.at[pl.ds(0, unit)],
            dst_ref=wdn.at[pl.ds(unit, unit)],
            send_sem=w_send.at[0],
            recv_sem=w_recv.at[0],
            device_id=partner,
            device_id_type=MESH,
        ),
        pltpu.make_async_remote_copy(
            src_ref=xu.at[pl.ds(rows, unit)],
            dst_ref=xu.at[pl.ds(rows + unit, unit)],
            send_sem=w_send.at[1],
            recv_sem=w_recv.at[1],
            device_id=partner,
            device_id_type=MESH,
        ),
    ]
    for copy in w_copies:
        copy.start()

    def gossip(q, src, dst, sem, which):
        return pltpu.make_async_remote_copy(
            src_ref=src,
            dst_ref=dst.at[p],
            send_sem=sem.at[2 * which],
            recv_sem=sem.at[2 * which + 1],
            device_id=(s, q, c),
            device_id_type=MESH,
        )

    def spread(src, dst, sem):
        size = dst.shape[1]

        def go(k, carry):
            q = peer_at(k)
            piece = src.at[pl.ds(pl.multiple_of(q * size, size), size)]
            gossip(q, piece, dst, sem, 0).start()
            return carry

        lax.fori_loop(0, others, go, 0)
        dst[p] = src[pl.ds(pl.multiple_of(p * size, size), size), :]

    def give_back(src, held, dst, sem):
        arrived_all(src.at[pl.ds(0, others)], sem.at[1])

        def swap(q, carry):
            m = mat[0, q]
            held[q] = src[m]
            return carry

        lax.fori_loop(0, peers, swap, 0)

        def go(k, carry):
            q = peer_at(k)
            gossip(q, held.at[q], dst, sem, 1).start()
            return carry

        lax.fori_loop(0, others, go, 0)
        dst[p] = held[p]

    spread(w1s, w1r, gw_sem)

    def cols(j):
        return pl.ds(pl.multiple_of(j * WIDE, WIDE), WIDE)

    def prepare(load):
        def body(j, acc):
            for t in range(WIDE // LANE):
                at = pl.ds(pl.multiple_of(j * WIDE + t * LANE, LANE), LANE)
                v = load(at).astype(F32)
                scaled[:, at] = (v * gain_v[:, at].astype(F32)).astype(BF16)
                acc = acc + v * v
            return acc

        acc = lax.fori_loop(0, steps, body, jnp.zeros((rows, LANE), F32))
        return 1.0 / jnp.sqrt(jnp.sum(acc, axis=-1, keepdims=True) / depth + norm_eps)

    loads[2].wait()
    loads[3].wait()
    r_f = prepare(lambda at: xu[pl.ds(0, rows), at])
    for copy in w_copies:
        copy.wait()
    pre_f = dot_nt(scaled[...], wdn[...]) * r_f
    act_f = (pre_f * sigmoid(pre_f)).astype(BF16)
    picked_f = dot_nn(hot_f[...], act_f).astype(BF16)
    mix_f = jnp.concatenate([hot_f[...], picked_f], axis=1)

    def chunk(h):
        return pl.ds(h * part, part)

    def route(k, h, pk, out, target, send, recv):
        q = peer_at(k)
        return pltpu.make_async_remote_copy(
            src_ref=pk.at[pl.ds(pl.multiple_of(q * cap, cap), cap), chunk(h)],
            dst_ref=out.at[pl.ds(pl.multiple_of(p * cap, cap), cap), chunk(h)],
            send_sem=send.at[h],
            recv_sem=recv.at[h],
            device_id=(target, q, c),
            device_id_type=MESH,
        )

    def handover(h, pk, target):
        return pltpu.make_async_remote_copy(
            src_ref=pk.at[:, chunk(h)],
            dst_ref=relay.at[h],
            send_sem=q_send.at[h],
            recv_sem=q_recv.at[h],
            device_id=(target, p, c),
            device_id_type=MESH,
        )

    def send_f(h):
        @pl.when(h < out_f_relays)
        def _():
            handover(min(h, RELAYS - 1), pk_f, nxt).start()

        @pl.when(has_next & (h >= out_f_relays))
        def _():
            def go(k, carry):
                route(k, h, pk_f, arrived, nxt, f_send, f_recv).start()
                return carry

            lax.fori_loop(0, peers, go, 0)

    def send_b(h):
        @pl.when(h < out_b_relays)
        def _():
            handover(min(h, RELAYS - 1), pk_b, prv).start()

        @pl.when(has_prev & (h >= out_b_relays))
        def _():
            def go(k, carry):
                route(k, h, pk_b, returned, prv, b_send, b_recv).start()
                return carry

            lax.fori_loop(0, peers, go, 0)

    def send_both(hf, hb):
        plain_f = has_next & (hf >= out_f_relays)
        plain_b = has_prev & (hb >= out_b_relays)

        def go(k, carry):
            @pl.when(plain_f)
            def _():
                route(k, hf, pk_f, arrived, nxt, f_send, f_recv).start()

            @pl.when(plain_b)
            def _():
                route(k, hb, pk_b, returned, prv, b_send, b_recv).start()

            return carry

        lax.fori_loop(0, peers, go, 0)

    for h in range(CHUNKS):
        for t in range(0, part, 256):
            at = pl.ds(h * part + t, 256)
            pk_f[:, at] = dot_nn(mix_f, xu[:, at]).astype(BF16)
        if h < 2:
            send_f(h)

    @pl.when(out_f_relays > 2)
    def _():
        handover(2, pk_f, nxt).start()

    loads[4].wait()
    loads[5].wait()
    slot_matrix(rcnt, hot_b)
    r_s = prepare(lambda at: y_v[:, at])
    pre_s = dot_nt(scaled[...], wdn[...]) * r_s
    grad_act = dot_nt(g_v[...], xu[pl.ds(rows, 2 * unit), :])
    sig = sigmoid(pre_s)
    act_s = (pre_s * sig).astype(BF16)
    grad_pre = grad_act * (sig * (1.0 + pre_s * (1.0 - sig)))
    pull = jnp.sum(grad_pre * pre_s, axis=-1, keepdims=True) * r_s * r_s / depth
    pre_r = (grad_pre * r_s).astype(BF16)

    def grads(j, carry):
        gu = dot_tn(act_s, g_v[:, cols(j)])
        gd = dot_tn(pre_r, scaled[:, cols(j)])
        part_own[0, :, cols(j)] = gd[:unit]
        part_out[0, :, cols(j)] = gd[unit:]
        part_own[1, :, cols(j)] = gu[:unit]
        part_out[1, :, cols(j)] = gu[unit:]
        return carry

    lax.fori_loop(0, steps, grads, 0)
    p_copy = pltpu.make_async_remote_copy(
        src_ref=part_out,
        dst_ref=part_in,
        send_sem=p_send,
        recv_sem=p_recv,
        device_id=partner,
        device_id_type=MESH,
    )
    p_copy.start()

    give_back(w1r, w2s, w2r, gw_sem)

    for h in range(CHUNKS):
        for t in range(0, part, 256):
            at = pl.ds(h * part + t, 256)
            u = dot_nn(pre_r, wdn[:, at]) * gain_v[:, at].astype(F32)
            v = g_v[:, at].astype(F32) + u - y_v[:, at].astype(F32) * pull
            pk_b[:, at] = dot_nn(hot_b[...], v.astype(BF16)).astype(BF16)
        if h < RELAYS:

            @pl.when(h < out_b_relays)
            def _():
                handover(h, pk_b, prv).start()

    for i in range(6, 10):
        loads[i].wait()
    p_copy.wait()

    def adam(j, carry):
        at = lanes(j)
        for i in range(2):
            grad = part_own[i, :, at] + part_in[i, :, at]
            m = beta_one * st[2 + i, :, at] + (1.0 - beta_one) * grad
            v = beta_two * st[4 + i, :, at] + (1.0 - beta_two) * grad * grad
            st[i, :, at] = stepped(st[i, :, at], m, v)
            st[2 + i, :, at] = m
            st[4 + i, :, at] = v
            m1s[tile(i, j), :] = m.astype(BF16)
            m1s[tile(2 + i, j), :] = v.astype(BF16)
        return carry

    lax.fori_loop(0, blocks, adam, 0)
    spread(m1s, m1r, gm_sem)

    send_both(2, 0)
    send_both(3, 1)

    def rest(k, carry):
        @pl.when(has_prev & (2 >= out_b_relays))
        def _():
            route(k, 2, pk_b, returned, prv, b_send, b_recv).start()

        @pl.when(has_prev)
        def _():
            route(k, 3, pk_b, returned, prv, b_send, b_recv).start()

        return carry

    lax.fori_loop(0, peers, rest, 0)

    @pl.when(s == 0)
    def _():
        zero[...] = jnp.zeros_like(zero)
        for h in range(CHUNKS):
            for q in range(peers):
                spot = arrived.at[pl.ds(q * cap, cap), chunk(h)]
                pltpu.make_async_copy(zero, spot, f_recv.at[h]).start()

    @pl.when(s == sections - 1)
    def _():
        zero[...] = jnp.zeros_like(zero)
        for h in range(CHUNKS):
            for q in range(peers):
                spot = returned.at[pl.ds(q * cap, cap), chunk(h)]
                pltpu.make_async_copy(zero, spot, b_recv.at[h]).start()

    def pass_on(h, out, recv):
        arrived_all(relay.at[h], q_recv.at[h])

        def go(k, carry):
            q = peer_at(k)
            pltpu.make_async_remote_copy(
                src_ref=relay.at[h, pl.ds(pl.multiple_of(q * cap, cap), cap)],
                dst_ref=out.at[pl.ds(pl.multiple_of(p * cap, cap), cap), chunk(h)],
                send_sem=l_send.at[h],
                recv_sem=recv.at[h],
                device_id=(s, q, c),
                device_id_type=MESH,
            ).start()
            return carry

        lax.fori_loop(0, others, go, 0)
        mine = pl.ds(pl.multiple_of(p * cap, cap), cap)
        pltpu.make_async_copy(relay.at[h, mine], out.at[mine, chunk(h)], recv.at[h]).start()

    for h in range(RELAYS):

        @pl.when(h < in_f_relays)
        def _():
            pass_on(h, arrived, f_recv)

        @pl.when(h < in_b_relays)
        def _():
            pass_on(h, returned, b_recv)

    give_back(m1r, m2s, m2r, gm_sem)

    arrived_all(w2r.at[pl.ds(0, others)], gw_sem.at[3])
    arrived_all(m2r.at[pl.ds(0, others)], gm_sem.at[3])

    def landed(ref, a, j):
        per = ref.shape[1] // unit
        t = a * blocks + j
        row = pl.multiple_of(lax.rem(t, per) * unit, unit)
        return ref[lax.div(t, per), pl.ds(row, unit), :].astype(F32)

    def average(j, carry):
        at = lanes(j)
        for i in range(2):
            m = landed(m2r, i, j)
            v = landed(m2r, 2 + i, j)
            w = stepped(landed(w2r, i, j), m, v)
            st[i, :, at] = (st[i, :, at] + w) * 0.5
            st[2 + i, :, at] = (st[2 + i, :, at] + m) * 0.5
            st[4 + i, :, at] = (st[4 + i, :, at] + v) * 0.5
        return carry

    lax.fori_loop(0, blocks, average, 0)
    stores = [pltpu.make_async_copy(st.at[a], outs[a], out_sem.at[a]) for a in range(6)]
    for store in stores:
        store.start()

    for ref, sem in ((w1r, gw_sem), (m1r, gm_sem)):
        arrived_all(ref.at[pl.ds(0, others)], sem.at[0])
        arrived_all(ref.at[pl.ds(0, others)], sem.at[2])
    for h in range(RELAYS):

        @pl.when((h < out_f_relays) | (h < out_b_relays))
        def _():
            arrived_all(relay.at[h], q_send.at[h])

        @pl.when((h < in_f_relays) | (h < in_b_relays))
        def _():
            arrived_all(relay.at[h, pl.ds(0, others * cap)], l_send.at[h])

    for h in range(CHUNKS):

        @pl.when(has_next & (h >= out_f_relays))
        def _():
            arrived_all(pk_f.at[:, chunk(h)], f_send.at[h])

        @pl.when(has_prev & (h >= out_b_relays))
        def _():
            arrived_all(pk_b.at[:, chunk(h)], b_send.at[h])

        arrived_all(arrived.at[:, chunk(h)], f_recv.at[h])
        arrived_all(returned.at[:, chunk(h)], b_recv.at[h])
    for store in stores:
        store.wait()


def settle(*refs):
    count = 8
    pieces = []
    for i in range(count):
        height = refs[i].shape[0]
        step = 32 if height > 32 else height
        for row in range(0, height, step):
            pieces.append((i, pl.ds(row, step)))
    holds = refs[2 * count : 3 * count]
    into, out = refs[3 * count :]
    reads = [
        pltpu.make_async_copy(refs[i].at[at], holds[i].at[at], into.at[n])
        for n, (i, at) in enumerate(pieces)
    ]
    writes = [
        pltpu.make_async_copy(holds[i].at[at], refs[count + i].at[at], out.at[n])
        for n, (i, at) in enumerate(pieces)
    ]
    for read in reads:
        read.start()
    for read, write in zip(reads, writes):
        read.wait()
        write.start()
    for write in writes:
        write.wait()


def local(sections, peers, near, *args):
    rows, depth = args[0].shape
    unit = args[7].shape[0]
    cap = 2 * rows // peers
    slots = peers * cap
    tiles = 2 * unit * depth // LANE
    any_spec = pl.BlockSpec(memory_space=pl.ANY)
    smem = pl.BlockSpec(memory_space=pltpu.SMEM)
    dma = pltpu.SemaphoreType.DMA
    shapes = [jax.ShapeDtypeStruct((slots, depth), BF16)] * 2 + [
        jax.ShapeDtypeStruct((unit, depth), F32)
    ] * 6

    def slabs(count):
        return pltpu.VMEM((peers, count * tiles // peers, LANE), BF16)

    results = pl.pallas_call(
        functools.partial(kernel, sections, peers, near),
        out_shape=shapes,
        in_specs=[any_spec] * 4 + [smem] * 3 + [any_spec] * 6,
        out_specs=[any_spec] * 8,
        scratch_shapes=[
            pltpu.VMEM((rows + 2 * unit, depth), BF16),
            pltpu.VMEM((2 * unit, depth), BF16),
            pltpu.VMEM((rows, depth), BF16),
            pltpu.VMEM((rows, depth), BF16),
            pltpu.VMEM((1, depth), BF16),
            pltpu.VMEM((6, unit, depth), F32),
            pltpu.VMEM((rows, depth), BF16),
            pltpu.VMEM((slots, depth), BF16),
            pltpu.VMEM((slots, depth), BF16),
            pltpu.VMEM((slots, rows), BF16),
            pltpu.VMEM((slots, rows), BF16),
            pltpu.VMEM((2, unit, depth), F32),
            pltpu.VMEM((2, unit, depth), F32),
            pltpu.VMEM((2, unit, depth), F32),
            pltpu.VMEM((tiles, LANE), BF16),
            slabs(1),
            slabs(1),
            slabs(1),
            pltpu.VMEM((2 * tiles, LANE), BF16),
            slabs(2),
            slabs(2),
            slabs(2),
            pltpu.VMEM((RELAYS, slots, depth // CHUNKS), BF16),
            pltpu.VMEM((cap, depth // CHUNKS), BF16),
            dma((10,)),
            dma((2,)),
            dma((2,)),
            dma,
            dma,
            dma((CHUNKS,)),
            dma((CHUNKS,)),
            dma((CHUNKS,)),
            dma((CHUNKS,)),
            dma((RELAYS,)),
            dma((RELAYS,)),
            dma((RELAYS,)),
            dma((4,)),
            dma((4,)),
            dma((6,)),
        ],
        compiler_params=pltpu.CompilerParams(
            collective_id=0, has_side_effects=True, vmem_limit_bytes=60 * 2**20
        ),
    )(*args)
    return pl.pallas_call(
        settle,
        out_shape=shapes,
        in_specs=[any_spec] * 8,
        out_specs=[any_spec] * 8,
        scratch_shapes=[pltpu.VMEM(shape.shape, shape.dtype) for shape in shapes]
        + [dma((2 * slots // 32 + 6,))] * 2,
        compiler_params=pltpu.CompilerParams(vmem_limit_bytes=60 * 2**20),
    )(*results)


def solution(mesh):
    sections, peers = mesh.shape["section"], mesh.shape["peer"]
    rows = P(AXES, None)
    by_section = P("section", None)
    return jax.shard_map(
        functools.partial(local, sections, peers, peers // 2),
        mesh=mesh,
        in_specs=(rows, rows, rows, by_section, rows, rows, by_section) + (rows,) * 6,
        out_specs=(rows,) * 8,
        check_vma=False,
    )
```

time: 225 us -> 167 us (0.74)
  the two profiles are of different devices: /device:TPU:140 before, /device:TPU:56 now
where the time goes in v2:
time: 167 us; the launch traced here: 163 us
  Pallas kernels  163 us (98%)
    pallas_call x1, Pallas kernels, local(): pl.pallas_call(functools.partial(kernel, sections, peers, near), out_shap...  157 us
    pallas_call x1, Pallas kernels, local(): pl.pallas_call(settle, out_shape=shapes, in_specs=[any_spec] * 8, out_spe...  5.9 us

profile of v2, /device:TPU:56, one launch (start us, length us, event | category | flops | bytes accessed | tf_op | source)
XLA Modules:
  0.0 163.3 jit_solution(15665338855380085495)
XLA Ops:
  0.6 156.7 %shard_map.188 = (bf16[256,5120]{1,0:T(8,128)(2,1)}, bf16[256,5120]{1,0:T(8,128)(2,1)}, f32[16,5120]{1,0:T(8,128)}, f32[16,5120]{1,0:T(8,128)}, f32[16,5120]{1,0...) custom-call(bf16[128,5120]{1,0:T(8,128)(2,1)} %x_hbm.1, bf16[128,5120]{1,0:T(8,128)(2,1)} %y_hbm.1, ...), custom_call_target="tpu_custom_call" | custom-call | tf_op jit(solution)/shard_map/pallas_call | solution.py:614
  157.3 5.9 %shard_map.189 = (bf16[256,5120]{1,0:T(8,128)(2,1)}, bf16[256,5120]{1,0:T(8,128)(2,1)}, f32[16,5120]{1,0:T(8,128)}, f32[16,5120]{1,0:T(8,128)}, f32[16,5120]{1,0...) custom-call(bf16[256,5120]{1,0:T(8,128)(2,1)} %get-tuple-element.16.refs_0_, ...), custom_call_target="tpu_custom_call" | custom-call | tf_op jit(solution)/shard_map/pallas_call | solution.py:664

commit v3 on v2

--- a/solution.py
+++ b/solution.py
@@ -12,7 +12,10 @@
 LANE = 128
 WIDE = 512
 CHUNKS = 4
-RELAYS = 3
+SHARE = CHUNKS // 4
+RELAYS = 3 * SHARE
+FIRST = 2
+TILE = 256
 beta_one = 0.9
 beta_two = 0.999
 learn_rate = 0.001
@@ -130,10 +133,10 @@
     nxt = s + 1
     prv = s - 1
     half = sections // 2
-    out_f_relays = jnp.where(has_next, jnp.maximum(s - (half - 1), 0), 0)
-    out_b_relays = jnp.where(has_prev, jnp.maximum(half - s, 0), 0)
-    in_f_relays = jnp.maximum(s - half, 0)
-    in_b_relays = jnp.maximum(half - 1 - s, 0)
+    out_f_relays = SHARE * jnp.where(has_next, jnp.maximum(s - (half - 1), 0), 0)
+    out_b_relays = SHARE * jnp.where(has_prev, jnp.maximum(half - s, 0), 0)
+    in_f_relays = SHARE * jnp.maximum(s - half, 0)
+    in_b_relays = SHARE * jnp.maximum(half - 1 - s, 0)
 
     px = p // near
     pz = lax.rem(p, near)
@@ -285,12 +288,13 @@
     def cols(j):
         return pl.ds(pl.multiple_of(j * WIDE, WIDE), WIDE)
 
-    def prepare(load):
+    def inverse(load, keep):
         def body(j, acc):
             for t in range(WIDE // LANE):
                 at = pl.ds(pl.multiple_of(j * WIDE + t * LANE, LANE), LANE)
                 v = load(at).astype(F32)
-                scaled[:, at] = (v * gain_v[:, at].astype(F32)).astype(BF16)
+                if keep:
+                    scaled[:, at] = (v * gain_v[:, at].astype(F32)).astype(BF16)
                 acc = acc + v * v
             return acc
 
@@ -299,7 +303,7 @@
 
     loads[2].wait()
     loads[3].wait()
-    r_f = prepare(lambda at: xu[pl.ds(0, rows), at])
+    r_f = inverse(lambda at: xu[pl.ds(0, rows), at], True)
     for copy in w_copies:
         copy.wait()
     pre_f = dot_nt(scaled[...], wdn[...]) * r_f
@@ -331,11 +335,17 @@
             device_id_type=MESH,
         )
 
+    def hand_f(h):
+        @pl.when(h < out_f_relays)
+        def _():
+            handover(h, pk_f, nxt).start()
+
+    def hand_b(h):
+        @pl.when(h < out_b_relays)
+        def _():
+            handover(h, pk_b, prv).start()
+
     def send_f(h):
-        @pl.when(h < out_f_relays)
-        def _():
-            handover(min(h, RELAYS - 1), pk_f, nxt).start()
-
         @pl.when(has_next & (h >= out_f_relays))
         def _():
             def go(k, carry):
@@ -345,10 +355,6 @@
             lax.fori_loop(0, peers, go, 0)
 
     def send_b(h):
-        @pl.when(h < out_b_relays)
-        def _():
-            handover(min(h, RELAYS - 1), pk_b, prv).start()
-
         @pl.when(has_prev & (h >= out_b_relays))
         def _():
             def go(k, carry):
@@ -375,31 +381,37 @@
         lax.fori_loop(0, peers, go, 0)
 
     for h in range(CHUNKS):
-        for t in range(0, part, 256):
-            at = pl.ds(h * part + t, 256)
+        for t in range(0, part, TILE):
+            at = pl.ds(h * part + t, TILE)
             pk_f[:, at] = dot_nn(mix_f, xu[:, at]).astype(BF16)
-        if h < 2:
+        if h < RELAYS:
+            hand_f(h)
+        if h < FIRST:
             send_f(h)
-
-    @pl.when(out_f_relays > 2)
-    def _():
-        handover(2, pk_f, nxt).start()
 
     loads[4].wait()
     loads[5].wait()
     slot_matrix(rcnt, hot_b)
-    r_s = prepare(lambda at: y_v[:, at])
-    pre_s = dot_nt(scaled[...], wdn[...]) * r_s
+    r_s = inverse(lambda at: y_v[:, at], False)
+
+    def normed(j, carry):
+        for t in range(WIDE // LANE):
+            at = pl.ds(pl.multiple_of(j * WIDE + t * LANE, LANE), LANE)
+            v = y_v[:, at].astype(F32) * r_s * gain_v[:, at].astype(F32)
+            scaled[:, at] = v.astype(BF16)
+        return carry
+
+    lax.fori_loop(0, steps, normed, 0)
+    pre_s = dot_nt(scaled[...], wdn[...])
     grad_act = dot_nt(g_v[...], xu[pl.ds(rows, 2 * unit), :])
     sig = sigmoid(pre_s)
     act_s = (pre_s * sig).astype(BF16)
-    grad_pre = grad_act * (sig * (1.0 + pre_s * (1.0 - sig)))
-    pull = jnp.sum(grad_pre * pre_s, axis=-1, keepdims=True) * r_s * r_s / depth
-    pre_r = (grad_pre * r_s).astype(BF16)
+    grad_pre = (grad_act * (sig * (1.0 + pre_s * (1.0 - sig)))).astype(BF16)
+    pull = jnp.sum(grad_pre.astype(F32) * pre_s, axis=-1, keepdims=True) * r_s * r_s / depth
 
     def grads(j, carry):
         gu = dot_tn(act_s, g_v[:, cols(j)])
-        gd = dot_tn(pre_r, scaled[:, cols(j)])
+        gd = dot_tn(grad_pre, scaled[:, cols(j)])
         part_own[0, :, cols(j)] = gd[:unit]
         part_out[0, :, cols(j)] = gd[unit:]
         part_own[1, :, cols(j)] = gu[:unit]
@@ -420,16 +432,13 @@
     give_back(w1r, w2s, w2r, gw_sem)
 
     for h in range(CHUNKS):
-        for t in range(0, part, 256):
-            at = pl.ds(h * part + t, 256)
-            u = dot_nn(pre_r, wdn[:, at]) * gain_v[:, at].astype(F32)
+        for t in range(0, part, TILE):
+            at = pl.ds(h * part + t, TILE)
+            u = dot_nn(grad_pre, wdn[:, at]) * gain_v[:, at].astype(F32) * r_s
             v = g_v[:, at].astype(F32) + u - y_v[:, at].astype(F32) * pull
             pk_b[:, at] = dot_nn(hot_b[...], v.astype(BF16)).astype(BF16)
         if h < RELAYS:
-
-            @pl.when(h < out_b_relays)
-            def _():
-                handover(h, pk_b, prv).start()
+            hand_b(h)
 
     for i in range(6, 10):
         loads[i].wait()
@@ -451,21 +460,11 @@
     lax.fori_loop(0, blocks, adam, 0)
     spread(m1s, m1r, gm_sem)
 
-    send_both(2, 0)
-    send_both(3, 1)
-
-    def rest(k, carry):
-        @pl.when(has_prev & (2 >= out_b_relays))
-        def _():
-            route(k, 2, pk_b, returned, prv, b_send, b_recv).start()
-
-        @pl.when(has_prev)
-        def _():
-            route(k, 3, pk_b, returned, prv, b_send, b_recv).start()
-
-        return carry
-
-    lax.fori_loop(0, peers, rest, 0)
+    for h in range(CHUNKS):
+        if FIRST + h < CHUNKS:
+            send_both(FIRST + h, h)
+        else:
+            send_b(h)
 
     @pl.when(s == 0)
     def _():
@@ -502,6 +501,8 @@
         mine = pl.ds(pl.multiple_of(p * cap, cap), cap)
         pltpu.make_async_copy(relay.at[h, mine], out.at[mine, chunk(h)], recv.at[h]).start()
 
+    give_back(m1r, m2s, m2r, gm_sem)
+
     for h in range(RELAYS):
 
         @pl.when(h < in_f_relays)
@@ -512,7 +513,6 @@
         def _():
             pass_on(h, returned, b_recv)
 
-    give_back(m1r, m2s, m2r, gm_sem)
 
     arrived_all(w2r.at[pl.ds(0, others)], gw_sem.at[3])
     arrived_all(m2r.at[pl.ds(0, others)], gm_sem.at[3])
@@ -570,29 +570,12 @@
 
 def settle(*refs):
     count = 8
-    pieces = []
-    for i in range(count):
-        height = refs[i].shape[0]
-        step = 32 if height > 32 else height
-        for row in range(0, height, step):
-            pieces.append((i, pl.ds(row, step)))
-    holds = refs[2 * count : 3 * count]
-    into, out = refs[3 * count :]
-    reads = [
-        pltpu.make_async_copy(refs[i].at[at], holds[i].at[at], into.at[n])
-        for n, (i, at) in enumerate(pieces)
-    ]
-    writes = [
-        pltpu.make_async_copy(holds[i].at[at], refs[count + i].at[at], out.at[n])
-        for n, (i, at) in enumerate(pieces)
-    ]
-    for read in reads:
-        read.start()
-    for read, write in zip(reads, writes):
-        read.wait()
-        write.start()
-    for write in writes:
-        write.wait()
+    sem = refs[-1]
+    copies = [pltpu.make_async_copy(refs[i], refs[count + i], sem.at[i]) for i in range(count)]
+    for copy in copies:
+        copy.start()
+    for copy in copies:
+        copy.wait()
 
 
 def local(sections, peers, near, *args):
@@ -611,9 +594,10 @@
     def slabs(count):
         return pltpu.VMEM((peers, count * tiles // peers, LANE), BF16)
 
+    args = [pltpu.with_memory_space_constraint(arg, pltpu.HBM) for arg in args]
     results = pl.pallas_call(
         functools.partial(kernel, sections, peers, near),
-        out_shape=shapes,
+        out_shape=[pltpu.VMEM(shape.shape, shape.dtype) for shape in shapes],
         in_specs=[any_spec] * 4 + [smem] * 3 + [any_spec] * 6,
         out_specs=[any_spec] * 8,
         scratch_shapes=[
@@ -658,7 +642,7 @@
             dma((6,)),
         ],
         compiler_params=pltpu.CompilerParams(
-            collective_id=0, has_side_effects=True, vmem_limit_bytes=60 * 2**20
+            collective_id=0, has_side_effects=True, vmem_limit_bytes=40 * 2**20
         ),
     )(*args)
     return pl.pallas_call(
@@ -666,9 +650,8 @@
         out_shape=shapes,
         in_specs=[any_spec] * 8,
         out_specs=[any_spec] * 8,
-        scratch_shapes=[pltpu.VMEM(shape.shape, shape.dtype) for shape in shapes]
-        + [dma((2 * slots // 32 + 6,))] * 2,
-        compiler_params=pltpu.CompilerParams(vmem_limit_bytes=60 * 2**20),
+        scratch_shapes=[dma((8,))],
+        compiler_params=pltpu.CompilerParams(vmem_limit_bytes=2 * 2**20),
     )(*results)
 
 

time: 167 us -> 160 us (0.958)
  Pallas kernels: 163 us -> 157 us
    pallas_call x1, Pallas kernels: 5.9 us -> 3.02 us  [local(): pl.pallas_call(settle, out_shape=shapes, in_specs=[any_spec] * 8, out_spe...]
    pallas_call x1, Pallas kernels: 157 us -> 154 us  [local(): pl.pallas_call(functools.partial(kernel, sections, peers, near), out_shap...]
where the time goes in v3:
time: 160 us; the launch traced here: 158 us
  Pallas kernels  157 us (98%)
    pallas_call x1, Pallas kernels, local(): pl.pallas_call(functools.partial(kernel, sections, peers, near), out_shap...  154 us

profile of v3, /device:TPU:56, one launch (start us, length us, event | category | flops | bytes accessed | tf_op | source)
XLA Modules:
  0.0 157.9 jit_solution(7024731133221267275)
XLA Ops:
  0.6 154.2 %shard_map.188 = (bf16[256,5120]{1,0:T(8,128)(2,1)S(1)}, bf16[256,5120]{1,0:T(8,128)(2,1)S(1)}, f32[16,5120]{1,0:T(8,128)S(1)}, f32[16,5120]{1,0:T(8,128)S(1)}, ...) custom-call(bf16[128,5120]{1,0:T(8,128)(2,1)} %x_hbm.1, ...), custom_call_target="tpu_custom_call" | custom-call | tf_op jit(solution)/shard_map/pallas_call | solution.py:598
  154.9 3.0 %shard_map.189 = (bf16[256,5120]{1,0:T(8,128)(2,1)}, bf16[256,5120]{1,0:T(8,128)(2,1)}, f32[16,5120]{1,0:T(8,128)}, f32[16,5120]{1,0:T(8,128)}, f32[16,5120]{1,0...) custom-call(bf16[256,5120]{1,0:T(8,128)(2,1)S(1)} %get-tuple-element.16.refs_0_, ...), custom_call_target="tpu_custom_call" | custom-call | tf_op jit(solution)/shard_map/pallas_call | solution.py:648

commit v4 on v3

--- a/solution.py
+++ b/solution.py
@@ -11,11 +11,12 @@
 AXES = ("section", "peer", "shard")
 LANE = 128
 WIDE = 512
-CHUNKS = 4
-SHARE = CHUNKS // 4
-RELAYS = 3 * SHARE
+F_SPANS = ((0, 10), (10, 10), (20, 10), (30, 10))
+B_SPANS = ((0, 2), (2, 10), (12, 10), (22, 10), (32, 8))
+F_RELAYS = 3
+B_RELAYS = 4
 FIRST = 2
-TILE = 256
+GROUP = 5
 beta_one = 0.9
 beta_two = 0.999
 learn_rate = 0.001
@@ -127,16 +128,15 @@
     cap = 2 * rows // peers
     steps = depth // WIDE
     blocks = depth // LANE
-    part = depth // CHUNKS
     has_next = s < sections - 1
     has_prev = s > 0
     nxt = s + 1
     prv = s - 1
     half = sections // 2
-    out_f_relays = SHARE * jnp.where(has_next, jnp.maximum(s - (half - 1), 0), 0)
-    out_b_relays = SHARE * jnp.where(has_prev, jnp.maximum(half - s, 0), 0)
-    in_f_relays = SHARE * jnp.maximum(s - half, 0)
-    in_b_relays = SHARE * jnp.maximum(half - 1 - s, 0)
+    out_f_relays = jnp.where(has_next, jnp.maximum(s - (half - 1), 0), 0)
+    in_f_relays = jnp.maximum(s - half, 0)
+    out_b_relays = jnp.where(has_prev, jnp.maximum(half + 1 - s, 0), 0)
+    in_b_relays = jnp.maximum(half - s, 0)
 
     px = p // near
     pz = lax.rem(p, near)
@@ -194,16 +194,18 @@
     loads[0].wait()
     loads[1].wait()
 
-    def cast(j, carry):
-        down = st[0, :, lanes(j)].astype(BF16)
-        up = st[1, :, lanes(j)].astype(BF16)
-        wdn[pl.ds(0, unit), lanes(j)] = down
-        xu[pl.ds(rows, unit), lanes(j)] = up
-        w1s[tile(0, j), :] = down
-        w1s[tile(1, j), :] = up
+    def cast(n, carry):
+        for t in range(GROUP):
+            j = n * GROUP + t
+            down = st[0, :, lanes(j)].astype(BF16)
+            up = st[1, :, lanes(j)].astype(BF16)
+            wdn[pl.ds(0, unit), lanes(j)] = down
+            xu[pl.ds(rows, unit), lanes(j)] = up
+            w1s[tile(0, j), :] = down
+            w1s[tile(1, j), :] = up
         return carry
 
-    lax.fori_loop(0, blocks, cast, 0)
+    lax.fori_loop(0, blocks // GROUP, cast, 0)
 
     row_id = lax.broadcasted_iota(jnp.int32, (cap, rows), 0)
     col_id = lax.broadcasted_iota(jnp.int32, (cap, rows), 1)
@@ -217,6 +219,32 @@
             offset = offset + n
 
     slot_matrix(fcnt, hot_f)
+
+    def cols(j):
+        return pl.ds(pl.multiple_of(j * WIDE, WIDE), WIDE)
+
+    def inverse(load):
+        def body(j, acc):
+            for t in range(WIDE // LANE):
+                v = load(pl.ds(pl.multiple_of(j * WIDE + t * LANE, LANE), LANE)).astype(F32)
+                acc = acc + v * v
+            return acc
+
+        acc = lax.fori_loop(0, steps, body, jnp.zeros((rows, LANE), F32))
+        return 1.0 / jnp.sqrt(jnp.sum(acc, axis=-1, keepdims=True) / depth + norm_eps)
+
+    def normalise(load, r):
+        def body(j, carry):
+            for t in range(WIDE // LANE):
+                at = pl.ds(pl.multiple_of(j * WIDE + t * LANE, LANE), LANE)
+                v = load(at).astype(F32) * r * gain_v[:, at].astype(F32)
+                scaled[:, at] = v.astype(BF16)
+            return carry
+
+        lax.fori_loop(0, steps, body, 0)
+
+    def forward_rows(at):
+        return xu[pl.ds(0, rows), at]
 
     groups = 1 + jnp.where(has_next, 1, 0) + jnp.where(has_prev, 1, 0)
     pl.semaphore_wait(barrier, peers * groups)
@@ -285,40 +313,26 @@
 
     spread(w1s, w1r, gw_sem)
 
-    def cols(j):
-        return pl.ds(pl.multiple_of(j * WIDE, WIDE), WIDE)
-
-    def inverse(load, keep):
-        def body(j, acc):
-            for t in range(WIDE // LANE):
-                at = pl.ds(pl.multiple_of(j * WIDE + t * LANE, LANE), LANE)
-                v = load(at).astype(F32)
-                if keep:
-                    scaled[:, at] = (v * gain_v[:, at].astype(F32)).astype(BF16)
-                acc = acc + v * v
-            return acc
-
-        acc = lax.fori_loop(0, steps, body, jnp.zeros((rows, LANE), F32))
-        return 1.0 / jnp.sqrt(jnp.sum(acc, axis=-1, keepdims=True) / depth + norm_eps)
-
     loads[2].wait()
     loads[3].wait()
-    r_f = inverse(lambda at: xu[pl.ds(0, rows), at], True)
+    normalise(forward_rows, inverse(forward_rows))
     for copy in w_copies:
         copy.wait()
-    pre_f = dot_nt(scaled[...], wdn[...]) * r_f
+    pre_f = dot_nt(scaled[...], wdn[...])
     act_f = (pre_f * sigmoid(pre_f)).astype(BF16)
     picked_f = dot_nn(hot_f[...], act_f).astype(BF16)
     mix_f = jnp.concatenate([hot_f[...], picked_f], axis=1)
 
-    def chunk(h):
-        return pl.ds(h * part, part)
+    def chunk(h, spans):
+        first, width = spans[h]
+        return pl.ds(first * LANE, width * LANE)
 
     def route(k, h, pk, out, target, send, recv):
         q = peer_at(k)
+        span = chunk(h, F_SPANS if pk is pk_f else B_SPANS)
         return pltpu.make_async_remote_copy(
-            src_ref=pk.at[pl.ds(pl.multiple_of(q * cap, cap), cap), chunk(h)],
-            dst_ref=out.at[pl.ds(pl.multiple_of(p * cap, cap), cap), chunk(h)],
+            src_ref=pk.at[pl.ds(pl.multiple_of(q * cap, cap), cap), span],
+            dst_ref=out.at[pl.ds(pl.multiple_of(p * cap, cap), cap), span],
             send_sem=send.at[h],
             recv_sem=recv.at[h],
             device_id=(target, q, c),
@@ -326,10 +340,11 @@
         )
 
     def handover(h, pk, target):
+        span = chunk(h, F_SPANS if pk is pk_f else B_SPANS)
         return pltpu.make_async_remote_copy(
-            src_ref=pk.at[:, chunk(h)],
-            dst_ref=relay.at[h],
-            send_sem=q_send.at[h],
+            src_ref=pk.at[:, span],
+            dst_ref=relay.at[:, span],
+            send_sem=q_send.at[h if pk is pk_f else len(F_SPANS) + h],
             recv_sem=q_recv.at[h],
             device_id=(target, p, c),
             device_id_type=MESH,
@@ -380,11 +395,11 @@
 
         lax.fori_loop(0, peers, go, 0)
 
-    for h in range(CHUNKS):
-        for t in range(0, part, TILE):
-            at = pl.ds(h * part + t, TILE)
+    for h, (first, width) in enumerate(F_SPANS):
+        for t in range(first, first + width, 2):
+            at = pl.ds(t * LANE, 2 * LANE)
             pk_f[:, at] = dot_nn(mix_f, xu[:, at]).astype(BF16)
-        if h < RELAYS:
+        if h < F_RELAYS:
             hand_f(h)
         if h < FIRST:
             send_f(h)
@@ -392,16 +407,8 @@
     loads[4].wait()
     loads[5].wait()
     slot_matrix(rcnt, hot_b)
-    r_s = inverse(lambda at: y_v[:, at], False)
-
-    def normed(j, carry):
-        for t in range(WIDE // LANE):
-            at = pl.ds(pl.multiple_of(j * WIDE + t * LANE, LANE), LANE)
-            v = y_v[:, at].astype(F32) * r_s * gain_v[:, at].astype(F32)
-            scaled[:, at] = v.astype(BF16)
-        return carry
-
-    lax.fori_loop(0, steps, normed, 0)
+    r_s = inverse(lambda at: y_v[:, at])
+    normalise(lambda at: y_v[:, at], r_s)
     pre_s = dot_nt(scaled[...], wdn[...])
     grad_act = dot_nt(g_v[...], xu[pl.ds(rows, 2 * unit), :])
     sig = sigmoid(pre_s)
@@ -431,22 +438,23 @@
 
     give_back(w1r, w2s, w2r, gw_sem)
 
-    for h in range(CHUNKS):
-        for t in range(0, part, TILE):
-            at = pl.ds(h * part + t, TILE)
+    for h, (first, width) in enumerate(B_SPANS):
+        for t in range(first, first + width, 2):
+            at = pl.ds(t * LANE, 2 * LANE)
             u = dot_nn(grad_pre, wdn[:, at]) * gain_v[:, at].astype(F32) * r_s
             v = g_v[:, at].astype(F32) + u - y_v[:, at].astype(F32) * pull
             pk_b[:, at] = dot_nn(hot_b[...], v.astype(BF16)).astype(BF16)
-        if h < RELAYS:
+        if h < B_RELAYS:
             hand_b(h)
 
     for i in range(6, 10):
         loads[i].wait()
     p_copy.wait()
 
-    def adam(j, carry):
-        at = lanes(j)
-        for i in range(2):
+    def adam(n, carry):
+        for i, t in ((i, t) for t in range(GROUP) for i in range(2)):
+            j = n * GROUP + t
+            at = lanes(j)
             grad = part_own[i, :, at] + part_in[i, :, at]
             m = beta_one * st[2 + i, :, at] + (1.0 - beta_one) * grad
             v = beta_two * st[4 + i, :, at] + (1.0 - beta_two) * grad * grad
@@ -457,11 +465,11 @@
             m1s[tile(2 + i, j), :] = v.astype(BF16)
         return carry
 
-    lax.fori_loop(0, blocks, adam, 0)
+    lax.fori_loop(0, blocks // GROUP, adam, 0)
     spread(m1s, m1r, gm_sem)
 
-    for h in range(CHUNKS):
-        if FIRST + h < CHUNKS:
+    for h in range(len(B_SPANS)):
+        if FIRST + h < len(F_SPANS):
             send_both(FIRST + h, h)
         else:
             send_b(h)
@@ -469,27 +477,29 @@
     @pl.when(s == 0)
     def _():
         zero[...] = jnp.zeros_like(zero)
-        for h in range(CHUNKS):
+        for h, (_, width) in enumerate(F_SPANS):
+            blank = zero.at[:, pl.ds(0, width * LANE)]
             for q in range(peers):
-                spot = arrived.at[pl.ds(q * cap, cap), chunk(h)]
-                pltpu.make_async_copy(zero, spot, f_recv.at[h]).start()
+                spot = arrived.at[pl.ds(q * cap, cap), chunk(h, F_SPANS)]
+                pltpu.make_async_copy(blank, spot, f_recv.at[h]).start()
 
     @pl.when(s == sections - 1)
     def _():
         zero[...] = jnp.zeros_like(zero)
-        for h in range(CHUNKS):
+        for h, (_, width) in enumerate(B_SPANS):
+            blank = zero.at[:, pl.ds(0, width * LANE)]
             for q in range(peers):
-                spot = returned.at[pl.ds(q * cap, cap), chunk(h)]
-                pltpu.make_async_copy(zero, spot, b_recv.at[h]).start()
-
-    def pass_on(h, out, recv):
-        arrived_all(relay.at[h], q_recv.at[h])
+                spot = returned.at[pl.ds(q * cap, cap), chunk(h, B_SPANS)]
+                pltpu.make_async_copy(blank, spot, b_recv.at[h]).start()
+
+    def pass_on(h, out, recv, span):
+        arrived_all(relay.at[:, span], q_recv.at[h])
 
         def go(k, carry):
             q = peer_at(k)
             pltpu.make_async_remote_copy(
-                src_ref=relay.at[h, pl.ds(pl.multiple_of(q * cap, cap), cap)],
-                dst_ref=out.at[pl.ds(pl.multiple_of(p * cap, cap), cap), chunk(h)],
+                src_ref=relay.at[pl.ds(pl.multiple_of(q * cap, cap), cap), span],
+                dst_ref=out.at[pl.ds(pl.multiple_of(p * cap, cap), cap), span],
                 send_sem=l_send.at[h],
                 recv_sem=recv.at[h],
                 device_id=(s, q, c),
@@ -499,20 +509,21 @@
 
         lax.fori_loop(0, others, go, 0)
         mine = pl.ds(pl.multiple_of(p * cap, cap), cap)
-        pltpu.make_async_copy(relay.at[h, mine], out.at[mine, chunk(h)], recv.at[h]).start()
+        pltpu.make_async_copy(relay.at[mine, span], out.at[mine, span], recv.at[h]).start()
 
     give_back(m1r, m2s, m2r, gm_sem)
 
-    for h in range(RELAYS):
+    for h in range(F_RELAYS):
 
         @pl.when(h < in_f_relays)
         def _():
-            pass_on(h, arrived, f_recv)
+            pass_on(h, arrived, f_recv, chunk(h, F_SPANS))
+
+    for h in range(B_RELAYS):
 
         @pl.when(h < in_b_relays)
         def _():
-            pass_on(h, returned, b_recv)
-
+            pass_on(h, returned, b_recv, chunk(h, B_SPANS))
 
     arrived_all(w2r.at[pl.ds(0, others)], gw_sem.at[3])
     arrived_all(m2r.at[pl.ds(0, others)], gm_sem.at[3])
@@ -523,49 +534,54 @@
         row = pl.multiple_of(lax.rem(t, per) * unit, unit)
         return ref[lax.div(t, per), pl.ds(row, unit), :].astype(F32)
 
-    def average(j, carry):
-        at = lanes(j)
-        for i in range(2):
+    def store(a, n):
+        at = pl.ds(pl.multiple_of(n * GROUP * LANE, GROUP * LANE), GROUP * LANE)
+        return pltpu.make_async_copy(st.at[a, :, at], outs[a].at[:, at], out_sem.at[a])
+
+    def average(n, carry):
+        for i, t in ((i, t) for t in range(GROUP) for i in range(2)):
+            j = n * GROUP + t
+            at = lanes(j)
             m = landed(m2r, i, j)
             v = landed(m2r, 2 + i, j)
             w = stepped(landed(w2r, i, j), m, v)
             st[i, :, at] = (st[i, :, at] + w) * 0.5
             st[2 + i, :, at] = (st[2 + i, :, at] + m) * 0.5
             st[4 + i, :, at] = (st[4 + i, :, at] + v) * 0.5
+        for a in range(6):
+            store(a, n).start()
         return carry
 
-    lax.fori_loop(0, blocks, average, 0)
-    stores = [pltpu.make_async_copy(st.at[a], outs[a], out_sem.at[a]) for a in range(6)]
-    for store in stores:
-        store.start()
+    lax.fori_loop(0, blocks // GROUP, average, 0)
 
     for ref, sem in ((w1r, gw_sem), (m1r, gm_sem)):
         arrived_all(ref.at[pl.ds(0, others)], sem.at[0])
         arrived_all(ref.at[pl.ds(0, others)], sem.at[2])
-    for h in range(RELAYS):
-
-        @pl.when((h < out_f_relays) | (h < out_b_relays))
-        def _():
-            arrived_all(relay.at[h], q_send.at[h])
-
-        @pl.when((h < in_f_relays) | (h < in_b_relays))
-        def _():
-            arrived_all(relay.at[h, pl.ds(0, others * cap)], l_send.at[h])
-
-    for h in range(CHUNKS):
-
-        @pl.when(has_next & (h >= out_f_relays))
-        def _():
-            arrived_all(pk_f.at[:, chunk(h)], f_send.at[h])
-
-        @pl.when(has_prev & (h >= out_b_relays))
-        def _():
-            arrived_all(pk_b.at[:, chunk(h)], b_send.at[h])
-
-        arrived_all(arrived.at[:, chunk(h)], f_recv.at[h])
-        arrived_all(returned.at[:, chunk(h)], b_recv.at[h])
-    for store in stores:
-        store.wait()
+    for spans, relays, out_relays, in_relays, pk, out, send, recv, on in (
+        (F_SPANS, F_RELAYS, out_f_relays, in_f_relays, pk_f, arrived, f_send, f_recv, has_next),
+        (B_SPANS, B_RELAYS, out_b_relays, in_b_relays, pk_b, returned, b_send, b_recv, has_prev),
+    ):
+        for h in range(len(spans)):
+            span = chunk(h, spans)
+            if h < relays:
+
+                @pl.when(h < out_relays)
+                def _():
+                    lane = h if pk is pk_f else len(F_SPANS) + h
+                    arrived_all(relay.at[:, span], q_send.at[lane])
+
+                @pl.when(h < in_relays)
+                def _():
+                    arrived_all(relay.at[pl.ds(0, others * cap), span], l_send.at[h])
+
+            @pl.when(on & (h >= out_relays))
+            def _():
+                arrived_all(pk.at[:, span], send.at[h])
+
+            arrived_all(out.at[:, span], recv.at[h])
+
+    for a in range(6):
+        arrived_all(st.at[a], out_sem.at[a])
 
 
 def settle(*refs):
@@ -623,20 +639,20 @@
             slabs(2),
             slabs(2),
             slabs(2),
-            pltpu.VMEM((RELAYS, slots, depth // CHUNKS), BF16),
-            pltpu.VMEM((cap, depth // CHUNKS), BF16),
+            pltpu.VMEM((slots, 32 * LANE), BF16),
+            pltpu.VMEM((cap, 10 * LANE), BF16),
             dma((10,)),
             dma((2,)),
             dma((2,)),
             dma,
             dma,
-            dma((CHUNKS,)),
-            dma((CHUNKS,)),
-            dma((CHUNKS,)),
-            dma((CHUNKS,)),
-            dma((RELAYS,)),
-            dma((RELAYS,)),
-            dma((RELAYS,)),
+            dma((4,)),
+            dma((4,)),
+            dma((5,)),
+            dma((5,)),
+            dma((8,)),
+            dma((4,)),
+            dma((4,)),
             dma((4,)),
             dma((4,)),
             dma((6,)),

time: 160 us -> 160 us (level)
  no operation moved by 1% of the time
where the time goes in v4:
time: 160 us; the launch traced here: 157 us
  Pallas kernels  156 us (98%)
    pallas_call x1, Pallas kernels, local(): pl.pallas_call(functools.partial(kernel, sections, peers, near), out_shap...  153 us

profile of v4, /device:TPU:56, one launch (start us, length us, event | category | flops | bytes accessed | tf_op | source)
XLA Modules:
  0.0 156.6 jit_solution(58910599705256159)
XLA Ops:
  0.6 153.0 %shard_map.188 = (bf16[256,5120]{1,0:T(8,128)(2,1)S(1)}, bf16[256,5120]{1,0:T(8,128)(2,1)S(1)}, f32[16,5120]{1,0:T(8,128)S(1)}, f32[16,5120]{1,0:T(8,128)S(1)}, ...) custom-call(bf16[128,5120]{1,0:T(8,128)(2,1)} %x_hbm.1, ...), custom_call_target="tpu_custom_call" | custom-call | tf_op jit(solution)/shard_map/pallas_call | solution.py:614
  153.6 3.0 %shard_map.189 = (bf16[256,5120]{1,0:T(8,128)(2,1)}, bf16[256,5120]{1,0:T(8,128)(2,1)}, f32[16,5120]{1,0:T(8,128)}, f32[16,5120]{1,0:T(8,128)}, f32[16,5120]{1,0...) custom-call(bf16[256,5120]{1,0:T(8,128)(2,1)S(1)} %get-tuple-element.16.refs_0_, ...), custom_call_target="tpu_custom_call" | custom-call | tf_op jit(solution)/shard_map/pallas_call | solution.py:664
